TPU v7x, 32 devices: a whole 2x2x4 slice. The times are simulated.
32 devices in a mesh: shots: 2 (over y), lat: 4 (over z), freq: 2 (over x), sub: 2 (over core).
Axes of the slice: x: 2, y: 2, z: 4, core: 2. Of those that a mesh axis runs over, the one named last changes fastest.
Arguments:
- wavefields: float32 [4, 4, 64, 1024], P(('shots', 'freq'), None, 'lat', 'sub'), parts along dimension 0, may hold values from -6 to 6
- velocity: float32 [8, 64, 1024], P('freq', 'lat', 'sub'), may hold values from 0 to 31
- filter_table: float32 [32, 32, 9, 2], replicated, may hold values from -1 to 1
- freq_pick: int32 [2], P('freq'), may hold values from 0 to 31
- slab_order: int32 [4], replicated, may hold values from 0 to 7
Outputs:
- fields_out: float32 [4, 4, 64, 1024], P(('shots', 'freq'), None, 'lat', 'sub'), parts along dimension 0
- image: float32 [8, 64, 1024], P(('shots', 'freq'), 'lat', 'sub'), parts along dimension 0
There are 2 independent parts, one for each index of `shots`. A program takes and returns all parts, laid end to end along the dimension named above; an argument that names none is the same for every part. Nothing has to cross between parts.
All inputs are finite; a program needn't handle non-finite values.
Results may differ from a plain program's by a relative error of at most 0.0003.
Values sent between devices are 32-bit elements; how exact they have to be, the bound alone decides.
A program may use at most 64 MiB of HBM per device.

v0:
```python
import jax
import jax.numpy as jnp
from jax import lax
from jax.sharding import PartitionSpec as P

KCHEB = 8
NBINS = 32
TABLE_FREQS = 32


def padded_2(cells, sides, width):
    for axis, dim in sides:
        count = lax.axis_size(axis)
        ends = count - 1
        head = lax.slice_in_dim(cells, 0, width, axis=dim)
        tail = lax.slice_in_dim(cells, cells.shape[dim] - width, cells.shape[dim], axis=dim)
        cells = jnp.concatenate(
            [
                lax.ppermute(tail, axis, [(i, (i + 1) % count) for i in range(ends)]),
                cells,
                lax.ppermute(head, axis, [((i + 1) % count, i) for i in range(ends)]),
            ],
            axis=dim,
        )
    return cells


def spread(value, axis, source):
    kept = jnp.where(lax.axis_index(axis) == source, value, 0).astype(value.dtype)
    return lax.psum(kept, axis)


def stencil(padded):
    edges = (
        padded[:, :, 2:, 1:-1]
        + padded[:, :, :-2, 1:-1]
        + padded[:, :, 1:-1, 2:]
        + padded[:, :, 1:-1, :-2]
    )
    corners = (
        padded[:, :, 2:, 2:]
        + padded[:, :, 2:, :-2]
        + padded[:, :, :-2, 2:]
        + padded[:, :, :-2, :-2]
    )
    return -0.5 * padded[:, :, 1:-1, 1:-1] + 0.25 * edges + 0.125 * corners


def combine(pair, term):
    real_part = pair[:, 0][:, None]
    imag_part = pair[:, 1][:, None]
    turned = jnp.stack([term[:, 1], -term[:, 0], -term[:, 3], term[:, 2]], axis=1)
    return real_part * term + imag_part * turned


def trim_edges(array, width):
    return array[:, :, width : array.shape[2] - width, width : array.shape[3] - width]


def propagate(fields, coefficients):
    rows_here = fields.shape[2]
    cols_here = fields.shape[3]
    padded = padded_2(fields, (("lat", 2), ("sub", 3)), KCHEB)
    row_ids = (
        lax.axis_index("lat") * rows_here
        - KCHEB
        + jnp.arange(rows_here + 2 * KCHEB, dtype=jnp.int32)
    )
    col_ids = (
        lax.axis_index("sub") * cols_here
        - KCHEB
        + jnp.arange(cols_here + 2 * KCHEB, dtype=jnp.int32)
    )
    row_inside = (row_ids >= 0) & (row_ids < rows_here * lax.axis_size("lat"))
    col_inside = (col_ids >= 0) & (col_ids < cols_here * lax.axis_size("sub"))
    inside = (row_inside[:, None] & col_inside[None, :]).astype(jnp.float32)[None, None]
    current = stencil(padded) * trim_edges(inside, 1)
    summed = combine(coefficients[:, 0], trim_edges(padded, KCHEB))
    summed = summed + combine(coefficients[:, 1], trim_edges(current, KCHEB - 1))
    previous = trim_edges(padded, 1)
    for order in range(2, KCHEB + 1):
        following = (2.0 * stencil(current) - trim_edges(previous, 1)) * trim_edges(inside, order)
        previous = trim_edges(current, 1)
        current = following
        summed = summed + combine(coefficients[:, order], trim_edges(current, KCHEB - order))
    return summed


def body(wavefields, velocity, filter_table, freq_pick, slab_order):
    highest = lax.Precision.HIGHEST
    freq_here = wavefields.shape[0]
    rows_here = wavefields.shape[2]
    cols_here = wavefields.shape[3]
    depth_count = slab_order.shape[0]
    slab_size = velocity.shape[0]
    onehot = (freq_pick[:, None] == jnp.arange(TABLE_FREQS, dtype=jnp.int32)[None, :]).astype(
        jnp.float32
    )
    selected = jnp.einsum("ft,btkc->bfkc", onehot, filter_table, precision=highest)
    selected = selected.reshape(NBINS, freq_here * (KCHEB + 1) * 2).T
    bin_grid = jnp.arange(NBINS, dtype=jnp.float32)[:, None]
    fields = wavefields
    images = []
    for depth_step in range(depth_count):
        stored_row = slab_order[depth_step]
        owner_index = stored_row // slab_size
        local_slab = lax.dynamic_index_in_dim(velocity, stored_row % slab_size, 0, keepdims=False)
        slowness = spread(local_slab, "freq", owner_index)
        weights = jnp.maximum(0.0, 1.0 - jnp.abs(slowness.reshape(1, -1) - bin_grid))
        coefficients = jnp.dot(
            selected, weights, precision=highest, preferred_element_type=jnp.float32
        )
        coefficients = coefficients.reshape(freq_here, KCHEB + 1, 2, rows_here, cols_here)
        fields = propagate(fields, coefficients)
        images.append(jnp.sum(fields[:, 0] * fields[:, 2] + fields[:, 1] * fields[:, 3], axis=0))
    image = lax.psum_scatter(jnp.stack(images), "freq", scatter_dimension=0, tiled=True)
    return (fields, image)


def solution(mesh):
    return jax.shard_map(
        body,
        mesh=mesh,
        in_specs=(
            P(("shots", "freq"), None, "lat", "sub"),
            P("freq", "lat", "sub"),
            P(),
            P("freq"),
            P(),
        ),
        out_specs=(P(("shots", "freq"), None, "lat", "sub"), P(("shots", "freq"), "lat", "sub")),
        check_vma=False,
    )
```

profile of v0, /device:TPU:0, one launch (start us, length us, event | category | flops | bytes accessed | tf_op | source)
XLA Modules:
  0.0 132.2 jit_solution(1288073521802857635)
XLA Ops:
  7.2 0.9 fusion.356
  8.2 1.4 %collective-permute-start.1 = (f32[1,4,8,512]{3,2,1,0:T(8,128)S(1)}, f32[1,4,8,512]{3,2,1,0:T(8,128)S(1)}, u32[]{:S(2)}, u32[]{:S(2)}) collective-permute-start(f32[1,4,8,512]{3,2,1,0:T(8,128)S(1)} %get-tuple-element.207), channel_id=1, source_target_pairs={{4,0},{8,4},{12,8},{5,1},{9,5},{13,9},{6,2},{10,6},{14,10},{7,3},{... | collective-permute-start | bytes 196616 | tf_op jit(solution)/shard_map/ppermute | solution.py:21
  9.6 5.6 %collective-permute-start = (f32[1,4,8,512]{3,2,1,0:T(8,128)S(1)}, f32[1,4,8,512]{3,2,1,0:T(8,128)S(1)}, u32[]{:S(2)}, u32[]{:S(2)}) collective-permute-start(f32[1,4,8,512]{3,2,1,0:T(8,128)S(1)} %get-tuple-element.208), channel_id=1, source_target_pairs={{0,4},{4,8},{8,12},{1,5},{5,9},{9,13},{2,6},{6,10},{10,14},{3,7},{... | collective-permute-start | bytes 196616 | tf_op jit(solution)/shard_map/ppermute | solution.py:19
  15.2 0.7 fusion.393
  26.1 0.7 select_bitcast_fusion.3
  27.6 0.7 copy-done.1
  28.3 0.6 fusion.355
  29.6 0.7 fusion.104
  30.5 1.5 %collective-permute-start.2 = (f32[1,4,32,8]{3,2,1,0:T(8,128)S(1)}, f32[1,4,32,8]{3,2,1,0:T(8,128)S(1)}, u32[]{:S(2)}, u32[]{:S(2)}) collective-permute-start(f32[1,4,32,8]{3,2,1,0:T(8,128)S(1)} %get-tuple-element.96), channel_id=1, source_target_pairs={{0,1},{2,3},{4,5},{6,7},{8,9},{10,11},{12,13},{14,15},{16,17},{18,... | collective-permute-start | bytes 12296 | tf_op jit(solution)/shard_map/ppermute | solution.py:19
  32.0 1.3 collective-permute-start.3
  33.4 1.7 %collective-permute-done.3 = f32[1,4,32,8]{3,2,1,0:T(8,128)S(1)} collective-permute-done((f32[1,4,32,8]{3,2,1,0:T(8,128)S(1)}, f32[1,4,32,8]{3,2,1,0:T(8,128)S(1)}, u32[]{:S(2)}, u32[]{:S(2)}) %collective-permute-start.3) | collective-permute-done | bytes 4128 | tf_op jit(solution)/shard_map/ppermute | solution.py:21
  35.9 0.7 fusion.93
  36.6 0.7 fusion.87
  38.9 0.7 fusion.345
  40.2 0.8 fusion.330
  41.3 0.8 fusion.347
  42.1 7.5 %all-reduce.3.cloned.1.call-done = (f32[16,512]{1,0:T(8,128)}, f32[16,512]{1,0:T(8,128)}, f32[16,512]{1,0:T(8,128)}, f32[16,512]{1,0:T(8,128)}) async-done(((f32[16,512]{1,0:T(8,128)}, f32[16,512]{1,0:T(8,128)}, f32[16,512]{1,0:T(8,128)}, f32[16,512]{1,0:T(8,128)}), (f32[16,512]{1,0:T(8,128)}, f32[16,512]{1,0:T(8,128)}, f32[16,512]{1,0:T(8,128)}, f32[16,512]{1,0:T(8,128)})) %all-reduce.3.cloned.1.call-update) | async-done | bytes 131088 | tf_op jit(solution)/shard_map/psum | solution.py:30
  49.6 1.8 %convolution_bitcast_fusion = f32[1,9,2,16,512]{4,1,3,2,0:T(8,128)S(1)} fusion(f32[16,512]{1,0:T(8,128)} %get-tuple-element.2, f32[9,2,32,1]{2,1,0,3:T(2,128)S(1)} %bitcast.356), kind=kOutput, calls=%fused_computation | convolution fusion | flops 57671680 | bytes 624896 | tf_op jit(solution)/shard_map/dot_general | solution.py:110
  53.7 3.4 %collective-permute-start.4 = (f32[1,4,8,512]{3,2,1,0:T(8,128)S(1)}, f32[1,4,8,512]{3,2,1,0:T(8,128)S(1)}, u32[]{:S(2)}, u32[]{:S(2)}) collective-permute-start(f32[1,4,8,512]{3,2,1,0:T(8,128)S(1)} %get-tuple-element.193), channel_id=1, source_target_pairs={{0,4},{4,8},{8,12},{1,5},{5,9},{9,13},{2,6},{6,10},{10,14},{3,7},{... | collective-permute-start | bytes 196616 | tf_op jit(solution)/shard_map/ppermute | solution.py:19
  57.1 1.5 %collective-permute-start.5 = (f32[1,4,8,512]{3,2,1,0:T(8,128)S(1)}, f32[1,4,8,512]{3,2,1,0:T(8,128)S(1)}, u32[]{:S(2)}, u32[]{:S(2)}) collective-permute-start(f32[1,4,8,512]{3,2,1,0:T(8,128)S(1)} %get-tuple-element.194), channel_id=1, source_target_pairs={{4,0},{8,4},{12,8},{5,1},{9,5},{13,9},{6,2},{10,6},{14,10},{7,3},{... | collective-permute-start | bytes 196616 | tf_op jit(solution)/shard_map/ppermute | solution.py:21
  58.6 1.0 convolution_bitcast_fusion.1
  60.2 0.7 copy-done.26
  60.9 1.0 convolution_bitcast_fusion.2
  62.4 0.7 copy-done.25
  63.2 1.0 convolution_bitcast_fusion.3
  65.1 1.3 collective-permute-start.6
  66.4 1.3 collective-permute-start.7
  67.9 1.6 %collective-permute-done.7 = f32[1,4,32,8]{3,2,1,0:T(8,128)S(1)} collective-permute-done((f32[1,4,32,8]{3,2,1,0:T(8,128)S(1)}, f32[1,4,32,8]{3,2,1,0:T(8,128)S(1)}, u32[]{:S(2)}, u32[]{:S(2)}) %collective-permute-start.7) | collective-permute-done | bytes 4128 | tf_op jit(solution)/shard_map/ppermute | solution.py:21
  70.3 0.7 fusion.76
  71.2 0.7 fusion.70
  75.3 4.5 %collective-permute-start.8 = (f32[1,4,8,512]{3,2,1,0:T(8,128)S(1)}, f32[1,4,8,512]{3,2,1,0:T(8,128)S(1)}, u32[]{:S(2)}, u32[]{:S(2)}) collective-permute-start(f32[1,4,8,512]{3,2,1,0:T(8,128)S(1)} %get-tuple-element.187), channel_id=1, source_target_pairs={{0,4},{4,8},{8,12},{1,5},{5,9},{9,13},{2,6},{6,10},{10,14},{3,7},{... | collective-permute-start | bytes 196616 | tf_op jit(solution)/shard_map/ppermute | solution.py:19
  79.8 1.3 collective-permute-start.9
  81.7 4.3 %collective-permute-done.9 = f32[1,4,8,512]{3,2,1,0:T(8,128)S(1)} collective-permute-done((f32[1,4,8,512]{3,2,1,0:T(8,128)S(1)}, f32[1,4,8,512]{3,2,1,0:T(8,128)S(1)}, u32[]{:S(2)}, u32[]{:S(2)}) %collective-permute-start.9) | collective-permute-done | bytes 65568 | tf_op jit(solution)/shard_map/ppermute | solution.py:21
  86.1 1.3 collective-permute-start.10
  87.4 1.5 %collective-permute-start.11 = (f32[1,4,32,8]{3,2,1,0:T(8,128)S(1)}, f32[1,4,32,8]{3,2,1,0:T(8,128)S(1)}, u32[]{:S(2)}, u32[]{:S(2)}) collective-permute-start(f32[1,4,32,8]{3,2,1,0:T(8,128)S(1)} %get-tuple-element.93), channel_id=1, source_target_pairs={{1,0},{3,2},{5,4},{7,6},{9,8},{11,10},{13,12},{15,14},{17,16},{19,... | collective-permute-start | bytes 12296 | tf_op jit(solution)/shard_map/ppermute | solution.py:21
  88.9 1.6 %collective-permute-done.11 = f32[1,4,32,8]{3,2,1,0:T(8,128)S(1)} collective-permute-done((f32[1,4,32,8]{3,2,1,0:T(8,128)S(1)}, f32[1,4,32,8]{3,2,1,0:T(8,128)S(1)}, u32[]{:S(2)}, u32[]{:S(2)}) %collective-permute-start.11) | collective-permute-done | bytes 4128 | tf_op jit(solution)/shard_map/ppermute | solution.py:21
  91.3 0.7 fusion.59
  92.1 0.7 fusion.53
  96.2 3.4 %collective-permute-start.12 = (f32[1,4,8,512]{3,2,1,0:T(8,128)S(1)}, f32[1,4,8,512]{3,2,1,0:T(8,128)S(1)}, u32[]{:S(2)}, u32[]{:S(2)}) collective-permute-start(f32[1,4,8,512]{3,2,1,0:T(8,128)S(1)} %get-tuple-element.181), channel_id=1, source_target_pairs={{0,4},{4,8},{8,12},{1,5},{5,9},{9,13},{2,6},{6,10},{10,14},{3,7},{... | collective-permute-start | bytes 196616 | tf_op jit(solution)/shard_map/ppermute | solution.py:19
  99.6 1.3 collective-permute-start.13
  101.5 4.3 %collective-permute-done.13 = f32[1,4,8,512]{3,2,1,0:T(8,128)S(1)} collective-permute-done((f32[1,4,8,512]{3,2,1,0:T(8,128)S(1)}, f32[1,4,8,512]{3,2,1,0:T(8,128)S(1)}, u32[]{:S(2)}, u32[]{:S(2)}) %collective-permute-start.13) | collective-permute-done | bytes 65568 | tf_op jit(solution)/shard_map/ppermute | solution.py:21
  105.9 1.3 collective-permute-start.14
  107.2 1.3 collective-permute-start.15
  108.5 1.8 %collective-permute-done.15 = f32[1,4,32,8]{3,2,1,0:T(8,128)S(1)} collective-permute-done((f32[1,4,32,8]{3,2,1,0:T(8,128)S(1)}, f32[1,4,32,8]{3,2,1,0:T(8,128)S(1)}, u32[]{:S(2)}, u32[]{:S(2)}) %collective-permute-start.15) | collective-permute-done | bytes 4128 | tf_op jit(solution)/shard_map/ppermute | solution.py:21
  111.1 0.7 fusion.42
  112.0 0.7 fusion.36
  116.1 0.7 pad_maximum_fusion.4
  116.8 8.6 %reduce-scatter.2.cloned.1.call-done = f32[2,16,512]{2,1,0:T(8,128)} async-done(((f32[4,16,512]{2,1,0:T(8,128)}), f32[2,16,512]{2,1,0:T(8,128)}) %reduce-scatter.2.cloned.1.call-update) | async-done | bytes 65552 | tf_op jit(solution)/shard_map/reduce_scatter | solution.py:116
  (245 shorter events, 22.0 us)
Async XLA Ops:
  7.2 22.4 %copy-start = (f32[32,32,9,2]{1,3,2,0:T(2,128)S(1)}, f32[32,32,9,2]{1,3,2,0:T(2,128)}, u32[]{:S(2)}) copy-start(f32[32,32,9,2]{1,3,2,0:T(2,128)} %param.7) | copy-start | bytes 221188
  7.2 42.4 %all-reduce.3.cloned.1.call-start = ((), (), s32[]{:S(2)}) async-start(), calls=%async_computation.2 | async-start | bytes 262144 | tf_op jit(solution)/shard_map/psum | solution.py:30
  7.2 8.0 %copy-start.28 = (s32[4]{0:T(128)S(1)}, s32[4]{0:T(128)}, u32[]{:S(2)}) copy-start(s32[4]{0:T(128)} %param.9) | copy-start | bytes 52
  8.2 18.0 %copy-start.24 = (f32[4,16,512]{2,1,0:T(8,128)S(1)}, f32[4,16,512]{2,1,0:T(8,128)}, u32[]{:S(2)}) copy-start(f32[4,16,512]{2,1,0:T(8,128)} %param.6) | copy-start | bytes 393220
  8.2 22.2 %collective-permute-start.1 = (f32[1,4,8,512]{3,2,1,0:T(8,128)S(1)}, f32[1,4,8,512]{3,2,1,0:T(8,128)S(1)}, u32[]{:S(2)}, u32[]{:S(2)}) collective-permute-start(f32[1,4,8,512]{3,2,1,0:T(8,128)S(1)} %get-tuple-element.207), channel_id=1, source_target_pairs={{4,0},{8,4},{12,8},{5,1},{9,5},{13,9},{6,2},{10,6},{14,10},{7,3},{... | collective-permute-start | bytes 196616 | tf_op jit(solution)/shard_map/ppermute | solution.py:21
  9.6 20.8 %collective-permute-start = (f32[1,4,8,512]{3,2,1,0:T(8,128)S(1)}, f32[1,4,8,512]{3,2,1,0:T(8,128)S(1)}, u32[]{:S(2)}, u32[]{:S(2)}) collective-permute-start(f32[1,4,8,512]{3,2,1,0:T(8,128)S(1)} %get-tuple-element.208), channel_id=1, source_target_pairs={{0,4},{4,8},{8,12},{1,5},{5,9},{9,13},{2,6},{6,10},{10,14},{3,7},{... | collective-permute-start | bytes 196616 | tf_op jit(solution)/shard_map/ppermute | solution.py:19
  26.8 98.5 %reduce-scatter.2.cloned.1.call-start = ((), (), s32[]{:S(2)}) async-start(), calls=%async_computation.1 | async-start | bytes 196608 | tf_op jit(solution)/shard_map/reduce_scatter | solution.py:116
  27.4 0.9 copy-start.1
  30.5 2.9 %collective-permute-start.2 = (f32[1,4,32,8]{3,2,1,0:T(8,128)S(1)}, f32[1,4,32,8]{3,2,1,0:T(8,128)S(1)}, u32[]{:S(2)}, u32[]{:S(2)}) collective-permute-start(f32[1,4,32,8]{3,2,1,0:T(8,128)S(1)} %get-tuple-element.96), channel_id=1, source_target_pairs={{0,1},{2,3},{4,5},{6,7},{8,9},{10,11},{12,13},{14,15},{16,17},{18,... | collective-permute-start | bytes 12296 | tf_op jit(solution)/shard_map/ppermute | solution.py:19
  32.0 3.1 %collective-permute-start.3 = (f32[1,4,32,8]{3,2,1,0:T(8,128)S(1)}, f32[1,4,32,8]{3,2,1,0:T(8,128)S(1)}, u32[]{:S(2)}, u32[]{:S(2)}) collective-permute-start(f32[1,4,32,8]{3,2,1,0:T(8,128)S(1)} %get-tuple-element.97), channel_id=1, source_target_pairs={{1,0},{3,2},{5,4},{7,6},{9,8},{11,10},{13,12},{15,14},{17,16},{19,... | collective-permute-start | bytes 12296 | tf_op jit(solution)/shard_map/ppermute | solution.py:21
  52.1 0.8 copy-start.18
  52.1 0.8 copy-start.19
  52.1 0.8 copy-start.20
  52.1 0.8 copy-start.21
  52.1 0.8 copy-start.22
  52.1 0.8 copy-start.23
  52.2 0.8 copy-start.16
  52.2 0.8 copy-start.17
  52.2 0.8 copy-start.14
  52.2 0.8 copy-start.15
  52.2 0.8 copy-start.12
  52.3 0.8 copy-start.13
  52.3 0.8 copy-start.10
  52.3 0.8 copy-start.11
  52.3 0.8 copy-start.6
  52.3 0.8 copy-start.7
  52.3 0.8 copy-start.8
  52.3 0.8 copy-start.9
  52.4 0.8 copy-start.5
  52.4 0.8 copy-start.3
  52.4 0.8 copy-start.4
  53.7 4.9 %copy-start.27 = (f32[16,512]{1,0:T(8,128)S(1)}, f32[16,512]{1,0:T(8,128)}, u32[]{:S(2)}) copy-start(f32[16,512]{1,0:T(8,128)} %get-tuple-element.3) | copy-start | bytes 98308
  53.7 11.3 %collective-permute-start.4 = (f32[1,4,8,512]{3,2,1,0:T(8,128)S(1)}, f32[1,4,8,512]{3,2,1,0:T(8,128)S(1)}, u32[]{:S(2)}, u32[]{:S(2)}) collective-permute-start(f32[1,4,8,512]{3,2,1,0:T(8,128)S(1)} %get-tuple-element.193), channel_id=1, source_target_pairs={{0,4},{4,8},{8,12},{1,5},{5,9},{9,13},{2,6},{6,10},{10,14},{3,7},{... | collective-permute-start | bytes 196616 | tf_op jit(solution)/shard_map/ppermute | solution.py:19
  57.1 7.9 %collective-permute-start.5 = (f32[1,4,8,512]{3,2,1,0:T(8,128)S(1)}, f32[1,4,8,512]{3,2,1,0:T(8,128)S(1)}, u32[]{:S(2)}, u32[]{:S(2)}) collective-permute-start(f32[1,4,8,512]{3,2,1,0:T(8,128)S(1)} %get-tuple-element.194), channel_id=1, source_target_pairs={{4,0},{8,4},{12,8},{5,1},{9,5},{13,9},{6,2},{10,6},{14,10},{7,3},{... | collective-permute-start | bytes 196616 | tf_op jit(solution)/shard_map/ppermute | solution.py:21
  60.1 0.8 copy-start.26
  62.4 0.8 copy-start.25
  65.1 2.8 %collective-permute-start.6 = (f32[1,4,32,8]{3,2,1,0:T(8,128)S(1)}, f32[1,4,32,8]{3,2,1,0:T(8,128)S(1)}, u32[]{:S(2)}, u32[]{:S(2)}) collective-permute-start(f32[1,4,32,8]{3,2,1,0:T(8,128)S(1)} %get-tuple-element.94), channel_id=1, source_target_pairs={{0,1},{2,3},{4,5},{6,7},{8,9},{10,11},{12,13},{14,15},{16,17},{18,... | collective-permute-start | bytes 12296 | tf_op jit(solution)/shard_map/ppermute | solution.py:19
  66.4 3.1 %collective-permute-start.7 = (f32[1,4,32,8]{3,2,1,0:T(8,128)S(1)}, f32[1,4,32,8]{3,2,1,0:T(8,128)S(1)}, u32[]{:S(2)}, u32[]{:S(2)}) collective-permute-start(f32[1,4,32,8]{3,2,1,0:T(8,128)S(1)} %get-tuple-element.95), channel_id=1, source_target_pairs={{1,0},{3,2},{5,4},{7,6},{9,8},{11,10},{13,12},{15,14},{17,16},{19,... | collective-permute-start | bytes 12296 | tf_op jit(solution)/shard_map/ppermute | solution.py:21
  75.3 6.4 %collective-permute-start.8 = (f32[1,4,8,512]{3,2,1,0:T(8,128)S(1)}, f32[1,4,8,512]{3,2,1,0:T(8,128)S(1)}, u32[]{:S(2)}, u32[]{:S(2)}) collective-permute-start(f32[1,4,8,512]{3,2,1,0:T(8,128)S(1)} %get-tuple-element.187), channel_id=1, source_target_pairs={{0,4},{4,8},{8,12},{1,5},{5,9},{9,13},{2,6},{6,10},{10,14},{3,7},{... | collective-permute-start | bytes 196616 | tf_op jit(solution)/shard_map/ppermute | solution.py:19
  79.8 6.2 %collective-permute-start.9 = (f32[1,4,8,512]{3,2,1,0:T(8,128)S(1)}, f32[1,4,8,512]{3,2,1,0:T(8,128)S(1)}, u32[]{:S(2)}, u32[]{:S(2)}) collective-permute-start(f32[1,4,8,512]{3,2,1,0:T(8,128)S(1)} %get-tuple-element.188), channel_id=1, source_target_pairs={{4,0},{8,4},{12,8},{5,1},{9,5},{13,9},{6,2},{10,6},{14,10},{7,3},{... | collective-permute-start | bytes 196616 | tf_op jit(solution)/shard_map/ppermute | solution.py:21
  86.1 2.8 %collective-permute-start.10 = (f32[1,4,32,8]{3,2,1,0:T(8,128)S(1)}, f32[1,4,32,8]{3,2,1,0:T(8,128)S(1)}, u32[]{:S(2)}, u32[]{:S(2)}) collective-permute-start(f32[1,4,32,8]{3,2,1,0:T(8,128)S(1)} %get-tuple-element.92), channel_id=1, source_target_pairs={{0,1},{2,3},{4,5},{6,7},{8,9},{10,11},{12,13},{14,15},{16,17},{18,... | collective-permute-start | bytes 12296 | tf_op jit(solution)/shard_map/ppermute | solution.py:19
  87.4 3.1 %collective-permute-start.11 = (f32[1,4,32,8]{3,2,1,0:T(8,128)S(1)}, f32[1,4,32,8]{3,2,1,0:T(8,128)S(1)}, u32[]{:S(2)}, u32[]{:S(2)}) collective-permute-start(f32[1,4,32,8]{3,2,1,0:T(8,128)S(1)} %get-tuple-element.93), channel_id=1, source_target_pairs={{1,0},{3,2},{5,4},{7,6},{9,8},{11,10},{13,12},{15,14},{17,16},{19,... | collective-permute-start | bytes 12296 | tf_op jit(solution)/shard_map/ppermute | solution.py:21
  96.2 5.3 %collective-permute-start.12 = (f32[1,4,8,512]{3,2,1,0:T(8,128)S(1)}, f32[1,4,8,512]{3,2,1,0:T(8,128)S(1)}, u32[]{:S(2)}, u32[]{:S(2)}) collective-permute-start(f32[1,4,8,512]{3,2,1,0:T(8,128)S(1)} %get-tuple-element.181), channel_id=1, source_target_pairs={{0,4},{4,8},{8,12},{1,5},{5,9},{9,13},{2,6},{6,10},{10,14},{3,7},{... | collective-permute-start | bytes 196616 | tf_op jit(solution)/shard_map/ppermute | solution.py:19
  99.6 6.2 %collective-permute-start.13 = (f32[1,4,8,512]{3,2,1,0:T(8,128)S(1)}, f32[1,4,8,512]{3,2,1,0:T(8,128)S(1)}, u32[]{:S(2)}, u32[]{:S(2)}) collective-permute-start(f32[1,4,8,512]{3,2,1,0:T(8,128)S(1)} %get-tuple-element.182), channel_id=1, source_target_pairs={{4,0},{8,4},{12,8},{5,1},{9,5},{13,9},{6,2},{10,6},{14,10},{7,3},{... | collective-permute-start | bytes 196616 | tf_op jit(solution)/shard_map/ppermute | solution.py:21
  105.9 2.6 %collective-permute-start.14 = (f32[1,4,32,8]{3,2,1,0:T(8,128)S(1)}, f32[1,4,32,8]{3,2,1,0:T(8,128)S(1)}, u32[]{:S(2)}, u32[]{:S(2)}) collective-permute-start(f32[1,4,32,8]{3,2,1,0:T(8,128)S(1)} %get-tuple-element.90), channel_id=1, source_target_pairs={{0,1},{2,3},{4,5},{6,7},{8,9},{10,11},{12,13},{14,15},{16,17},{18,... | collective-permute-start | bytes 12296 | tf_op jit(solution)/shard_map/ppermute | solution.py:19
  107.2 3.1 %collective-permute-start.15 = (f32[1,4,32,8]{3,2,1,0:T(8,128)S(1)}, f32[1,4,32,8]{3,2,1,0:T(8,128)S(1)}, u32[]{:S(2)}, u32[]{:S(2)}) collective-permute-start(f32[1,4,32,8]{3,2,1,0:T(8,128)S(1)} %get-tuple-element.91), channel_id=1, source_target_pairs={{1,0},{3,2},{5,4},{7,6},{9,8},{11,10},{13,12},{15,14},{17,16},{19,... | collective-permute-start | bytes 12296 | tf_op jit(solution)/shard_map/ppermute | solution.py:21
  116.0 0.7 copy-start.2
Sparse Core Ops, SparseCore 0:
  26.9 22.5 all-reduce.2
  116.9 8.4 reduce-scatter.1
where the time goes:
time: 133 us; the launch traced here: 132 us
  starting transfers between devices  33.2 us (25%)
  waiting for transfers between devices  32.2 us (24%)
  between operations  26.7 us (20%)
  other arithmetic  26.5 us (20%)
  local copies, waits for them, and re-layouts  7.93 us (6%)
  matrix products  5.61 us (4%)
    ppermute x8, starting transfers between devices, padded_2(): lax.ppermute(tail, axis, [(i, (i + 1) % count) for i in range(ends)])  22.2 us
    ppermute x8, waiting for transfers between devices, padded_2(): lax.ppermute(head, axis, [((i + 1) % count, i) for i in range(ends)])  15.3 us
    mul x28, other arithmetic, propagate(): (2.0 * stencil(current) - trim_edges(previous, 1)) * trim_edges(inside, o...  14.8 us
    ppermute x8, starting transfers between devices, padded_2(): lax.ppermute(head, axis, [((i + 1) % count, i) for i in range(ends)])  10.9 us
    reduce_scatter x1, waiting for transfers between devices, body(): lax.psum_scatter(jnp.stack(images), 'freq', scatter_dimension=0, tiled=True)  8.58 us
    psum x1, waiting for transfers between devices, spread(): return lax.psum(kept, axis)  7.53 us
    slice x29, other arithmetic, combine(): term[:, 1]  5.18 us
    dot_general x4, matrix products, body(): jnp.dot(selected, weights, precision=highest, preferred_element_type=jnp....  4.92 us
  transfers between devices with their start and end apart: 18, of which 10 were waited for; matrix products, arithmetic and copies ran while one was open for 12% of the time, Pallas kernels for 0%

commit v1 on v0

v1 whole, which is shorter than its diff:
```python
import functools

import jax
import jax.numpy as jnp
from jax import lax
from jax.experimental import pallas as pl
from jax.experimental.pallas import tpu as pltpu
from jax.sharding import PartitionSpec as P

KCHEB = 8
ORDERS = KCHEB + 1
HALO = 8
LANES = 128
MESH = pl.DeviceIdType.MESH


def kernel(sizes, wave_ref, vel_ref, tab_ref, slab_ref, out_ref, image_ref,
           fields, slots, coef, partial, arrived,
           halo_send, halo_recv, vel_send, vel_recv, img_send, img_recv):
    lats, freqs, bins = sizes
    depths = slab_ref.shape[0]
    slab_size, rows, cols = vel_ref.shape
    tiles = cols // LANES
    per = image_ref.shape[0]
    tall = rows + 2 * HALO
    lat = lax.axis_index("lat")
    sub = lax.axis_index("sub")
    freq = lax.axis_index("freq")
    has_up = lat > 0
    has_down = lat < lats - 1
    other = 1 - sub
    edge_tile = (tiles - 1) * (1 - sub)

    barrier = pltpu.get_barrier_semaphore()

    def greet(target):
        pl.semaphore_signal(barrier, inc=1, device_id=target, device_id_type=MESH)

    greet({"sub": other})
    for step in range(1, freqs):
        greet({"freq": lax.rem(freq + step, freqs)})

    @pl.when(has_up)
    def _():
        greet({"lat": lat - 1})
        greet({"lat": lat - 1, "sub": other})

    @pl.when(has_down)
    def _():
        greet({"lat": lat + 1})
        greet({"lat": lat + 1, "sub": other})

    pl.semaphore_wait(
        barrier, freqs + jnp.where(has_up, 2, 0) + jnp.where(has_down, 2, 0)
    )

    def vel_copy(d, source, target):
        return pltpu.make_async_remote_copy(
            src_ref=slots.at[d, source],
            dst_ref=slots.at[d, source],
            send_sem=vel_send.at[d, target],
            recv_sem=vel_recv.at[d, source],
            device_id={"freq": target},
            device_id_type=MESH,
        )

    def halo_copy(d, pair, way):
        src_rows = {0: HALO, 1: rows, 2: HALO, 3: HALO, 4: rows}[way]
        dst_rows = {0: HALO + rows, 1: 0, 2: HALO, 3: HALO + rows, 4: 0}[way]
        count = rows if way == 2 else HALO
        src_tiles, dst_tiles = (
            (pl.ds(0, tiles), pl.ds(0, tiles))
            if way < 2
            else (pl.ds(edge_tile, 1), pl.ds(tiles, 1))
        )
        target = {}
        if way in (0, 3):
            target["lat"] = lat - 1
        if way in (1, 4):
            target["lat"] = lat + 1
        if way >= 2:
            target["sub"] = other
        parts = pl.ds(2 * pair, 2)
        return pltpu.make_async_remote_copy(
            src_ref=fields.at[d, parts, src_tiles, pl.ds(src_rows, count)],
            dst_ref=fields.at[d, parts, dst_tiles, pl.ds(dst_rows, count)],
            send_sem=halo_send.at[d, pair, way],
            recv_sem=halo_recv.at[d, pair, way],
            device_id=target,
            device_id_type=MESH,
        )

    def send_halo(d, pair):
        @pl.when(has_up)
        def _():
            halo_copy(d, pair, 0).start()
            halo_copy(d, pair, 3).start()

        @pl.when(has_down)
        def _():
            halo_copy(d, pair, 1).start()
            halo_copy(d, pair, 4).start()

        halo_copy(d, pair, 2).start()

    def wait_halo(d, pair):
        halo_copy(d, pair, 2).wait_recv()

        @pl.when(has_down)
        def _():
            halo_copy(d, pair, 0).wait_recv()
            halo_copy(d, pair, 3).wait_recv()

        @pl.when(has_up)
        def _():
            halo_copy(d, pair, 1).wait_recv()
            halo_copy(d, pair, 4).wait_recv()

    def wait_halo_sent(d, pair):
        @pl.when(has_up)
        def _():
            halo_copy(d, pair, 0).wait_send()
            halo_copy(d, pair, 3).wait_send()

        @pl.when(has_down)
        def _():
            halo_copy(d, pair, 1).wait_send()
            halo_copy(d, pair, 4).wait_send()

        halo_copy(d, pair, 2).wait_send()

    for pair in range(2):
        for part in (2 * pair, 2 * pair + 1):
            for t in range(tiles):
                fields[0, part, t, pl.ds(HALO, rows)] = wave_ref[0, part, :, t * LANES:(t + 1) * LANES]
        send_halo(0, pair)
        for d in range(depths) if pair == 0 else ():
            slots[d, freq] = vel_ref[slab_ref[d] % slab_size]
            for step in range(1, freqs):
                vel_copy(d, freq, lax.rem(freq + step, freqs)).start()

    lane = lax.broadcasted_iota(jnp.int32, (tall, LANES), 1)
    row = lax.broadcasted_iota(jnp.int32, (tall, LANES), 0)
    row_low = jnp.where(has_up, 0, HALO)
    row_high = jnp.where(has_down, tall, tall - HALO)
    row_mask = (row >= row_low) & (row < row_high)
    lane_low = jnp.where(sub == 0, 0, LANES // 2)
    halo_mask = row_mask & (lane >= lane_low) & (lane < lane_low + LANES // 2)
    first_lane = lane == 0
    last_lane = lane == LANES - 1

    def make_coefficients(d):
        for step in range(1, freqs):
            source = lax.rem(freq + step, freqs)
            vel_copy(d, source, source).wait_recv()
        owner = slab_ref[d] // slab_size
        for t in range(tiles):
            for r in range(0, rows, 8):
                v = jnp.zeros((8, LANES), jnp.float32)
                for source in range(freqs):
                    block = slots[d, source, r:r + 8, t * LANES:(t + 1) * LANES]
                    v = jnp.where(owner == source, block, v)
                base = jnp.floor(v)
                upper = v - base
                lower = 1.0 - upper
                index = jnp.clip(base.astype(jnp.int32), 0, bins - 1)
                index_next = jnp.minimum(index + 1, bins - 1)
                for j in range(ORDERS * 2):
                    start = j * bins
                    window, shift = start // LANES, start % LANES
                    table = jnp.broadcast_to(
                        tab_ref[0:1, window * LANES:(window + 1) * LANES], (8, LANES)
                    )
                    low = jnp.take_along_axis(table, index + shift, axis=1, mode="promise_in_bounds")
                    high = jnp.take_along_axis(table, index_next + shift, axis=1, mode="promise_in_bounds")
                    coef[j, t, pl.ds(r, 8)] = low * lower + high * upper

    def smooth(xs):
        ys = []
        for x in xs:
            w = x + pltpu.roll(x, tall - 1, 0)
            ys.append(w + pltpu.roll(w, 1, 0))
        n = len(ys)
        left = [pltpu.roll(y, LANES - 1, 1) for y in ys]
        ws = [ys[t] + jnp.where(last_lane, left[(t + 1) % n], left[t]) for t in range(n)]
        right = [pltpu.roll(w, 1, 1) for w in ws]
        return [ws[t] + jnp.where(first_lane, right[t - 1], right[t]) for t in range(n)]

    def masked(xs):
        return [jnp.where(row_mask if t < tiles else halo_mask, x, 0.0) for t, x in enumerate(xs)]

    def propagate(d, pair):
        sign = 1.0 if pair == 0 else -1.0
        now = [
            masked([fields[d, 2 * pair + part, t] for t in range(tiles + 1)]) for part in range(2)
        ]
        before = None
        total = [[None] * tiles for _ in range(2)]
        for k in range(ORDERS):
            if k > 0:
                new = []
                for part in range(2):
                    sums = smooth(now[part])
                    if k == 1:
                        xs = [0.125 * s - x for s, x in zip(sums, now[part])]
                    else:
                        xs = [
                            0.25 * s - (2.0 * x + y)
                            for s, x, y in zip(sums, now[part], before[part])
                        ]
                    new.append(masked(xs) if k < KCHEB else xs)
                before, now = now, new
            for t in range(tiles):
                a = coef[2 * k, t]
                b = coef[2 * k + 1, t]
                p = now[0][t][HALO:HALO + rows]
                q = now[1][t][HALO:HALO + rows]
                if pair == 0:
                    add0, add1 = a * p + b * q, a * q - b * p
                else:
                    add0, add1 = a * p - b * q, a * q + b * p
                total[0][t] = add0 if k == 0 else total[0][t] + add0
                total[1][t] = add1 if k == 0 else total[1][t] + add1
        for part in range(2):
            for t in range(tiles):
                fields[d + 1, 2 * pair + part, t, pl.ds(HALO, rows)] = total[part][t]

    def image_copy(d, source, owner):
        return pltpu.make_async_remote_copy(
            src_ref=partial.at[d],
            dst_ref=arrived.at[d, source],
            send_sem=img_send.at[d],
            recv_sem=img_recv.at[d, source],
            device_id={"freq": owner},
            device_id_type=MESH,
        )

    make_coefficients(0)

    def depth_step(d, carry):
        for pair in range(2):
            wait_halo(d, pair)
            propagate(d, pair)

            @pl.when(d < depths - 1)
            def _():
                send_halo(d + 1, pair)

        for t in range(tiles):
            u = [fields[d + 1, part, t, pl.ds(HALO, rows)] for part in range(4)]
            partial[d, :, t * LANES:(t + 1) * LANES] = u[0] * u[2] + u[1] * u[3]
        owner = d // per

        @pl.when(owner != freq)
        def _():
            image_copy(d, freq, owner).start()

        @pl.when(d < depths - 1)
        def _():
            make_coefficients(d + 1)

        return carry

    lax.fori_loop(0, depths, depth_step, 0)

    for part in range(4):
        for t in range(tiles):
            out_ref[0, part, :, t * LANES:(t + 1) * LANES] = fields[depths, part, t, pl.ds(HALO, rows)]

    for i in range(per):
        d = freq * per + i
        total = partial[d]
        for step in range(1, freqs):
            source = lax.rem(freq + step, freqs)
            image_copy(d, source, source).wait_recv()
            total = total + arrived[d, source]
        image_ref[i] = total

    for d in range(depths):
        for pair in range(2):
            wait_halo_sent(d, pair)
        for step in range(1, freqs):
            vel_copy(d, freq, lax.rem(freq + step, freqs)).wait_send()

        @pl.when(d // per != freq)
        def _():
            image_copy(d, freq, d // per).wait_send()


def body(sizes, wavefields, velocity, filter_table, freq_pick, slab_order):
    lats, freqs = sizes
    depths = slab_order.shape[0]
    _, parts, rows, cols = wavefields.shape
    tiles = cols // LANES
    bins = filter_table.shape[0]
    per = depths // freqs
    table = lax.dynamic_index_in_dim(filter_table, freq_pick[0], 1, keepdims=False)
    table = jnp.transpose(table, (1, 2, 0)).reshape(1, ORDERS * 2 * bins)
    wide = -(-table.shape[1] // LANES) * LANES
    table = jnp.pad(table, ((0, 0), (0, wide - table.shape[1])))
    vmem = pl.BlockSpec(memory_space=pltpu.VMEM)
    return pl.pallas_call(
        functools.partial(kernel, (lats, freqs, bins)),
        out_shape=(
            jax.ShapeDtypeStruct(wavefields.shape, jnp.float32),
            jax.ShapeDtypeStruct((per, rows, cols), jnp.float32),
        ),
        in_specs=[vmem, vmem, vmem, pl.BlockSpec(memory_space=pltpu.SMEM)],
        out_specs=(vmem, vmem),
        scratch_shapes=[
            pltpu.VMEM((depths + 1, parts, tiles + 1, rows + 2 * HALO, LANES), jnp.float32),
            pltpu.VMEM((depths, freqs, rows, cols), jnp.float32),
            pltpu.VMEM((ORDERS * 2, tiles, rows, LANES), jnp.float32),
            pltpu.VMEM((depths, rows, cols), jnp.float32),
            pltpu.VMEM((depths, freqs, rows, cols), jnp.float32),
            pltpu.SemaphoreType.DMA((depths, 2, 5)),
            pltpu.SemaphoreType.DMA((depths, 2, 5)),
            pltpu.SemaphoreType.DMA((depths, freqs)),
            pltpu.SemaphoreType.DMA((depths, freqs)),
            pltpu.SemaphoreType.DMA((depths,)),
            pltpu.SemaphoreType.DMA((depths, freqs)),
        ],
        compiler_params=pltpu.CompilerParams(
            collective_id=0, has_side_effects=True, vmem_limit_bytes=32 * 1024 * 1024
        ),
    )(wavefields, velocity, table, slab_order)


def solution(mesh):
    sizes = (mesh.shape["lat"], mesh.shape["freq"])
    return jax.shard_map(
        functools.partial(body, sizes),
        mesh=mesh,
        in_specs=(
            P(("shots", "freq"), None, "lat", "sub"),
            P("freq", "lat", "sub"),
            P(),
            P("freq"),
            P(),
        ),
        out_specs=(P(("shots", "freq"), None, "lat", "sub"), P(("shots", "freq"), "lat", "sub")),
        check_vma=False,
    )
```

time: 133 us -> 32.2 us (0.24)
  starting transfers between devices: 33.2 us -> 0 us
  waiting for transfers between devices: 32.2 us -> 0 us
  Pallas kernels: 0 us -> 27.8 us
  other arithmetic: 26.5 us -> 0 us
  between operations: 26.7 us -> 1.37 us
  matrix products: 5.61 us -> 0 us
  local copies, waits for them, and re-layouts: 7.93 us -> 2.9 us
    ppermute x16 -> x0, starting transfers between devices: 33.1 us -> none  [the longest x8 22.2 us: padded_2(): lax.ppermute(tail, axis, [(i, (i + 1) % count) for i in range(ends)])]
    pallas_call x0 -> x1, Pallas kernels: none -> 27.8 us  [body(): pl.pallas_call(functools.partial(kernel, (lats, freqs, bins)), out_shape=...]
    mul x32 -> x0, other arithmetic: 17.1 us -> none  [the longest x28 14.8 us: propagate(): (2.0 * stencil(current) - trim_edges(previous, 1)) * trim_edges(inside, o...]
    ppermute x16 -> x0, waiting for transfers between devices: 16.1 us -> none  [the longest x8 15.3 us: padded_2(): lax.ppermute(head, axis, [((i + 1) % count, i) for i in range(ends)])]
    reduce_scatter x1 -> x0, waiting for transfers between devices: 8.58 us -> none  [body(): lax.psum_scatter(jnp.stack(images), 'freq', scatter_dimension=0, tiled=True)]
    psum x1 -> x0, waiting for transfers between devices: 7.53 us -> none  [spread(): return lax.psum(kept, axis)]
    dot_general x5 -> x0, matrix products: 5.61 us -> none  [the longest x4 4.92 us: body(): jnp.dot(selected, weights, precision=highest, preferred_element_type=jnp....]
    slice x32 -> x0, other arithmetic: 5.43 us -> none  [the longest x29 5.18 us: combine(): term[:, 1]]
  transfers between devices with their start and end apart: 18 -> 0, of which waited for: 10 -> 0; matrix products, arithmetic and copies ran while one was open for 12% -> 0% of each run, Pallas kernels for 0% -> 0%
where the time goes in v1:
time: 32.2 us; the launch traced here: 32 us
  Pallas kernels  27.8 us (86%)
  local copies, waits for them, and re-layouts  2.9 us (9%)
  between operations  1.37 us (4%)
    pallas_call x1, Pallas kernels, body(): pl.pallas_call(functools.partial(kernel, (lats, freqs, bins)), out_shape=...  27.8 us
    unnamed x10, local copies, waits for them, and re-layouts  2.24 us

profile of v1, /device:TPU:0, one launch (start us, length us, event | category | flops | bytes accessed | tf_op | source)
XLA Modules:
  0.0 32.0 jit_solution(13099791392440915897)
XLA Ops:
  0.6 0.0 copy-start
  1.3 0.3 copy-done
  1.6 0.4 %constant_dynamic-slice_fusion = f32[32,1,9,2]{1,3,2,0:T(2,128)S(1)} fusion(f32[32,32,9,2]{1,3,2,0:T(2,128)S(1)} %copy-done, s32[]{:T(128)S(6)} %select_n.4), kind=kLoop, calls=%fused_computation | loop fusion | bytes 4612 | tf_op jit(solution)/shard_map/jit(dynamic_index_in_dim)/dynamic_slice | solution.py:297
  2.0 0.0 copy-start.1
  2.0 0.0 copy-start.2
  2.0 0.2 copy.7
  2.2 0.1 reshape.7
  2.3 0.0 copy-start.3
  2.3 0.6 %copy-done.1 = f32[1,4,16,512]{3,2,1,0:T(8,128)S(1)} copy-done((f32[1,4,16,512]{3,2,1,0:T(8,128)S(1)}, f32[1,4,16,512]{3,2,1,0:T(8,128)}, u32[]{:S(2)}) %copy-start.1) | copy-done | bytes 131096
  2.9 0.1 copy-done.2
  3.0 0.0 copy-done.3
  3.0 27.8 %shard_map.68 = (f32[1,4,16,512]{3,2,1,0:T(8,128)S(1)}, f32[2,16,512]{2,1,0:T(8,128)S(1)}) custom-call(f32[1,4,16,512]{3,2,1,0:T(8,128)S(1)} %copy-done.1, f32[4,16,512]{2,1,0:T(8,128)S(1)} %copy-done.2, f32[1,640]{1,0:T(1,128)S(1)} %pad.4.tab_ref, s32[4]{0:T(128)S(1)} %copy-done.3), custom_call_target="tpu_custom_call" | custom-call | tf_op jit(solution)/shard_map/pallas_call | solution.py:302
  30.8 0.7 %copy.11 = f32[1,4,16,512]{3,2,1,0:T(8,128)} copy(f32[1,4,16,512]{3,2,1,0:T(8,128)S(1)} %get-tuple-element.4) | data formatting | bytes 262144
  31.4 0.6 %copy.12 = f32[2,16,512]{2,1,0:T(8,128)} copy(f32[2,16,512]{2,1,0:T(8,128)S(1)} %get-tuple-element.5) | data formatting | bytes 131072
  (1 shorter events, 0.0 us)
Async XLA Ops:
  0.6 1.0 %copy-start = (f32[32,32,9,2]{1,3,2,0:T(2,128)S(1)}, f32[32,32,9,2]{1,3,2,0:T(2,128)}, u32[]{:S(2)}) copy-start(f32[32,32,9,2]{1,3,2,0:T(2,128)} %param.7) | copy-start | bytes 221188
  2.0 0.9 %copy-start.1 = (f32[1,4,16,512]{3,2,1,0:T(8,128)S(1)}, f32[1,4,16,512]{3,2,1,0:T(8,128)}, u32[]{:S(2)}) copy-start(f32[1,4,16,512]{3,2,1,0:T(8,128)} %wave_ref.1) | copy-start | bytes 393220
  2.0 1.0 %copy-start.2 = (f32[4,16,512]{2,1,0:T(8,128)S(1)}, f32[4,16,512]{2,1,0:T(8,128)}, u32[]{:S(2)}) copy-start(f32[4,16,512]{2,1,0:T(8,128)} %vel_ref.1) | copy-start | bytes 393220
  2.3 0.7 %copy-start.3 = (s32[4]{0:T(128)S(1)}, s32[4]{0:T(128)}, u32[]{:S(2)}) copy-start(s32[4]{0:T(128)} %slab_ref.1) | copy-start | bytes 52

commit v2 on v1

--- a/solution.py
+++ b/solution.py
@@ -15,7 +15,7 @@
 
 
 def kernel(sizes, wave_ref, vel_ref, tab_ref, slab_ref, out_ref, image_ref,
-           fields, slots, coef, partial, arrived,
+           fields, slots, coef, partial, arrived, work,
            halo_send, halo_recv, vel_send, vel_recv, img_send, img_recv):
     lats, freqs, bins = sizes
     depths = slab_ref.shape[0]
@@ -175,16 +175,22 @@
                     high = jnp.take_along_axis(table, index_next + shift, axis=1, mode="promise_in_bounds")
                     coef[j, t, pl.ds(r, 8)] = low * lower + high * upper
 
-    def smooth(xs):
+    def smooth(xs, k, parity, pair, part):
+        shift = parity * 8
         ys = []
-        for x in xs:
-            w = x + pltpu.roll(x, tall - 1, 0)
-            ys.append(w + pltpu.roll(w, 1, 0))
+        for t, x in enumerate(xs):
+            line = work.at[k % 2, 2 * pair + part, t]
+            line[pl.ds(pl.multiple_of(shift + 8, 8), tall)] = x
+            ys.append(line[pl.ds(shift + 7, tall)] + line[pl.ds(shift + 9, tall)] + (x + x))
         n = len(ys)
         left = [pltpu.roll(y, LANES - 1, 1) for y in ys]
-        ws = [ys[t] + jnp.where(last_lane, left[(t + 1) % n], left[t]) for t in range(n)]
-        right = [pltpu.roll(w, 1, 1) for w in ws]
-        return [ws[t] + jnp.where(first_lane, right[t - 1], right[t]) for t in range(n)]
+        right = [pltpu.roll(y, 1, 1) for y in ys]
+        return [
+            (ys[t] + ys[t])
+            + jnp.where(last_lane, left[(t + 1) % n], left[t])
+            + jnp.where(first_lane, right[t - 1], right[t])
+            for t in range(n)
+        ]
 
     def masked(xs):
         return [jnp.where(row_mask if t < tiles else halo_mask, x, 0.0) for t, x in enumerate(xs)]
@@ -200,7 +206,7 @@
             if k > 0:
                 new = []
                 for part in range(2):
-                    sums = smooth(now[part])
+                    sums = smooth(now[part], k, lax.rem(d, 2), pair, part)
                     if k == 1:
                         xs = [0.125 * s - x for s, x in zip(sums, now[part])]
                     else:
@@ -313,6 +319,7 @@
             pltpu.VMEM((ORDERS * 2, tiles, rows, LANES), jnp.float32),
             pltpu.VMEM((depths, rows, cols), jnp.float32),
             pltpu.VMEM((depths, freqs, rows, cols), jnp.float32),
+            pltpu.VMEM((2, parts, tiles + 1, rows + 2 * HALO + 24, LANES), jnp.float32),
             pltpu.SemaphoreType.DMA((depths, 2, 5)),
             pltpu.SemaphoreType.DMA((depths, 2, 5)),
             pltpu.SemaphoreType.DMA((depths, freqs)),

time: 32.2 us -> 30.3 us (0.941)
  Pallas kernels: 27.8 us -> 25.9 us
    pallas_call x1, Pallas kernels: 27.8 us -> 25.9 us  [body(): pl.pallas_call(functools.partial(kernel, (lats, freqs, bins)), out_shape=...]
where the time goes in v2:
time: 30.3 us; the launch traced here: 30.1 us
  Pallas kernels  25.9 us (85%)
  local copies, waits for them, and re-layouts  2.9 us (10%)
  between operations  1.37 us (5%)
    pallas_call x1, Pallas kernels, body(): pl.pallas_call(functools.partial(kernel, (lats, freqs, bins)), out_shape=...  25.9 us
    unnamed x10, local copies, waits for them, and re-layouts  2.24 us

profile of v2, /device:TPU:0, one launch (start us, length us, event | category | flops | bytes accessed | tf_op | source)
XLA Modules:
  0.0 30.1 jit_solution(12072774017190959916)
XLA Ops:
  0.6 0.0 copy-start
  1.3 0.3 copy-done
  1.6 0.4 %constant_dynamic-slice_fusion = f32[32,1,9,2]{1,3,2,0:T(2,128)S(1)} fusion(f32[32,32,9,2]{1,3,2,0:T(2,128)S(1)} %copy-done, s32[]{:T(128)S(6)} %select_n.4), kind=kLoop, calls=%fused_computation | loop fusion | bytes 4612 | tf_op jit(solution)/shard_map/jit(dynamic_index_in_dim)/dynamic_slice | solution.py:303
  2.0 0.0 copy-start.1
  2.0 0.0 copy-start.2
  2.0 0.2 copy.7
  2.2 0.1 reshape.7
  2.3 0.0 copy-start.3
  2.3 0.6 %copy-done.1 = f32[1,4,16,512]{3,2,1,0:T(8,128)S(1)} copy-done((f32[1,4,16,512]{3,2,1,0:T(8,128)S(1)}, f32[1,4,16,512]{3,2,1,0:T(8,128)}, u32[]{:S(2)}) %copy-start.1) | copy-done | bytes 131096
  2.9 0.1 copy-done.2
  3.0 0.0 copy-done.3
  3.0 25.9 %shard_map.68 = (f32[1,4,16,512]{3,2,1,0:T(8,128)S(1)}, f32[2,16,512]{2,1,0:T(8,128)S(1)}) custom-call(f32[1,4,16,512]{3,2,1,0:T(8,128)S(1)} %copy-done.1, f32[4,16,512]{2,1,0:T(8,128)S(1)} %copy-done.2, f32[1,640]{1,0:T(1,128)S(1)} %pad.4.tab_ref, s32[4]{0:T(128)S(1)} %copy-done.3), custom_call_target="tpu_custom_call" | custom-call | tf_op jit(solution)/shard_map/pallas_call | solution.py:308
  28.8 0.7 %copy.11 = f32[1,4,16,512]{3,2,1,0:T(8,128)} copy(f32[1,4,16,512]{3,2,1,0:T(8,128)S(1)} %get-tuple-element.4) | data formatting | bytes 262144
  29.5 0.6 %copy.12 = f32[2,16,512]{2,1,0:T(8,128)} copy(f32[2,16,512]{2,1,0:T(8,128)S(1)} %get-tuple-element.5) | data formatting | bytes 131072
  (1 shorter events, 0.0 us)
Async XLA Ops:
  0.6 1.0 %copy-start = (f32[32,32,9,2]{1,3,2,0:T(2,128)S(1)}, f32[32,32,9,2]{1,3,2,0:T(2,128)}, u32[]{:S(2)}) copy-start(f32[32,32,9,2]{1,3,2,0:T(2,128)} %param.7) | copy-start | bytes 221188
  2.0 0.9 %copy-start.1 = (f32[1,4,16,512]{3,2,1,0:T(8,128)S(1)}, f32[1,4,16,512]{3,2,1,0:T(8,128)}, u32[]{:S(2)}) copy-start(f32[1,4,16,512]{3,2,1,0:T(8,128)} %wave_ref.1) | copy-start | bytes 393220
  2.0 1.0 %copy-start.2 = (f32[4,16,512]{2,1,0:T(8,128)S(1)}, f32[4,16,512]{2,1,0:T(8,128)}, u32[]{:S(2)}) copy-start(f32[4,16,512]{2,1,0:T(8,128)} %vel_ref.1) | copy-start | bytes 393220
  2.3 0.7 %copy-start.3 = (s32[4]{0:T(128)S(1)}, s32[4]{0:T(128)}, u32[]{:S(2)}) copy-start(s32[4]{0:T(128)} %slab_ref.1) | copy-start | bytes 52

commit v3 on v1

--- a/solution.py
+++ b/solution.py
@@ -15,8 +15,8 @@
 
 
 def kernel(sizes, wave_ref, vel_ref, tab_ref, slab_ref, out_ref, image_ref,
-           fields, slots, coef, partial, arrived,
-           halo_send, halo_recv, vel_send, vel_recv, img_send, img_recv):
+           fields, slots, coef, partial, arrived, tables,
+           halo_send, halo_recv, vel_send, vel_recv, img_send, img_recv, *work):
     lats, freqs, bins = sizes
     depths = slab_ref.shape[0]
     slab_size, rows, cols = vel_ref.shape
@@ -49,10 +49,6 @@
     def _():
         greet({"lat": lat + 1})
         greet({"lat": lat + 1, "sub": other})
-
-    pl.semaphore_wait(
-        barrier, freqs + jnp.where(has_up, 2, 0) + jnp.where(has_down, 2, 0)
-    )
 
     def vel_copy(d, source, target):
         return pltpu.make_async_remote_copy(
@@ -129,15 +125,27 @@
 
         halo_copy(d, pair, 2).wait_send()
 
+    for d in range(depths):
+        slots[d, freq] = vel_ref[slab_ref[d] % slab_size]
+    for part in range(4):
+        for t in range(tiles):
+            fields[0, part, t, pl.ds(HALO, rows)] = wave_ref[0, part, :, t * LANES:(t + 1) * LANES]
+    pl.semaphore_wait(
+        barrier, freqs + jnp.where(has_up, 2, 0) + jnp.where(has_down, 2, 0)
+    )
+
+    for step in range(1, freqs):
+        vel_copy(0, freq, lax.rem(freq + step, freqs)).start()
     for pair in range(2):
-        for part in (2 * pair, 2 * pair + 1):
-            for t in range(tiles):
-                fields[0, part, t, pl.ds(HALO, rows)] = wave_ref[0, part, :, t * LANES:(t + 1) * LANES]
         send_halo(0, pair)
-        for d in range(depths) if pair == 0 else ():
-            slots[d, freq] = vel_ref[slab_ref[d] % slab_size]
-            for step in range(1, freqs):
-                vel_copy(d, freq, lax.rem(freq + step, freqs)).start()
+    for d in range(1, depths):
+        for step in range(1, freqs):
+            vel_copy(d, freq, lax.rem(freq + step, freqs)).start()
+    bin_id = lax.broadcasted_iota(jnp.int32, (8, LANES), 1)
+    for j in range(ORDERS * 2):
+        low = jnp.broadcast_to(tab_ref[j:j + 1], (8, LANES))
+        tables[2 * j] = low
+        tables[2 * j + 1] = jnp.where(bin_id < bins - 1, pltpu.roll(low, LANES - 1, 1) - low, 0.0)
 
     lane = lax.broadcasted_iota(jnp.int32, (tall, LANES), 1)
     row = lax.broadcasted_iota(jnp.int32, (tall, LANES), 0)
@@ -146,8 +154,8 @@
     row_mask = (row >= row_low) & (row < row_high)
     lane_low = jnp.where(sub == 0, 0, LANES // 2)
     halo_mask = row_mask & (lane >= lane_low) & (lane < lane_low + LANES // 2)
-    first_lane = lane == 0
-    last_lane = lane == LANES - 1
+    first_lane = lane[:8] == 0
+    last_lane = lane[:8] == LANES - 1
 
     def make_coefficients(d):
         for step in range(1, freqs):
@@ -162,68 +170,93 @@
                     v = jnp.where(owner == source, block, v)
                 base = jnp.floor(v)
                 upper = v - base
-                lower = 1.0 - upper
                 index = jnp.clip(base.astype(jnp.int32), 0, bins - 1)
-                index_next = jnp.minimum(index + 1, bins - 1)
                 for j in range(ORDERS * 2):
-                    start = j * bins
-                    window, shift = start // LANES, start % LANES
-                    table = jnp.broadcast_to(
-                        tab_ref[0:1, window * LANES:(window + 1) * LANES], (8, LANES)
-                    )
-                    low = jnp.take_along_axis(table, index + shift, axis=1, mode="promise_in_bounds")
-                    high = jnp.take_along_axis(table, index_next + shift, axis=1, mode="promise_in_bounds")
-                    coef[j, t, pl.ds(r, 8)] = low * lower + high * upper
-
-    def smooth(xs):
-        ys = []
-        for x in xs:
-            w = x + pltpu.roll(x, tall - 1, 0)
-            ys.append(w + pltpu.roll(w, 1, 0))
-        n = len(ys)
-        left = [pltpu.roll(y, LANES - 1, 1) for y in ys]
-        ws = [ys[t] + jnp.where(last_lane, left[(t + 1) % n], left[t]) for t in range(n)]
-        right = [pltpu.roll(w, 1, 1) for w in ws]
-        return [ws[t] + jnp.where(first_lane, right[t - 1], right[t]) for t in range(n)]
-
-    def masked(xs):
-        return [jnp.where(row_mask if t < tiles else halo_mask, x, 0.0) for t, x in enumerate(xs)]
+                    low = jnp.take_along_axis(tables[2 * j], index, axis=1, mode="promise_in_bounds")
+                    rise = jnp.take_along_axis(tables[2 * j + 1], index, axis=1, mode="promise_in_bounds")
+                    coef[j, t, pl.ds(r, 8)] = low + upper * rise
+
+    def kept(x, r, t):
+        rows_here = slice(r, r + 8)
+        if t == tiles:
+            return jnp.where(halo_mask[rows_here], x, 0.0)
+        if r < HALO or r >= HALO + rows:
+            return jnp.where(row_mask[rows_here], x, 0.0)
+        return x
 
     def propagate(d, pair):
-        sign = 1.0 if pair == 0 else -1.0
-        now = [
-            masked([fields[d, 2 * pair + part, t] for t in range(tiles + 1)]) for part in range(2)
-        ]
-        before = None
-        total = [[None] * tiles for _ in range(2)]
-        for k in range(ORDERS):
-            if k > 0:
+        shift = lax.rem(d, 2) * 8
+
+        def load(k, part, t, r, off=0):
+            start = shift + (8 + r + off)
+            if off == 0:
+                start = pl.multiple_of(start, 8)
+            return work[((k % 3) * 2 + part) * (tiles + 1) + t][pl.ds(start, 8)]
+
+        def store(k, part, t, r, x):
+            start = pl.multiple_of(shift + (8 + r), 8)
+            work[((k % 3) * 2 + part) * (tiles + 1) + t][pl.ds(start, 8)] = x
+
+        blocks = range(0, tall, 8)
+        centre = range(HALO, HALO + rows, 8)
+        total = [{} for _ in range(2)]
+
+        def add(k, t, r, now):
+            a = coef[2 * k, t, r - HALO:r - HALO + 8]
+            b = coef[2 * k + 1, t, r - HALO:r - HALO + 8]
+            p, q = now
+            if pair == 0:
+                add0, add1 = a * p + b * q, a * q - b * p
+            else:
+                add0, add1 = a * p - b * q, a * q + b * p
+            total[0][t, r] = add0 if k == 0 else total[0][t, r] + add0
+            total[1][t, r] = add1 if k == 0 else total[1][t, r] + add1
+
+        for r in blocks:
+            for t in range(tiles + 1):
+                now = []
+                for part in range(2):
+                    x = kept(fields[d, 2 * pair + part, t, r:r + 8], r, t)
+                    store(0, part, t, r, x)
+                    now.append(x)
+                if t < tiles and r in centre:
+                    add(0, t, r, now)
+        for k in range(1, ORDERS):
+            for r in blocks if k < KCHEB else centre:
                 new = []
                 for part in range(2):
-                    sums = smooth(now[part])
-                    if k == 1:
-                        xs = [0.125 * s - x for s, x in zip(sums, now[part])]
-                    else:
-                        xs = [
-                            0.25 * s - (2.0 * x + y)
-                            for s, x, y in zip(sums, now[part], before[part])
-                        ]
-                    new.append(masked(xs) if k < KCHEB else xs)
-                before, now = now, new
-            for t in range(tiles):
-                a = coef[2 * k, t]
-                b = coef[2 * k + 1, t]
-                p = now[0][t][HALO:HALO + rows]
-                q = now[1][t][HALO:HALO + rows]
-                if pair == 0:
-                    add0, add1 = a * p + b * q, a * q - b * p
-                else:
-                    add0, add1 = a * p - b * q, a * q + b * p
-                total[0][t] = add0 if k == 0 else total[0][t] + add0
-                total[1][t] = add1 if k == 0 else total[1][t] + add1
+                    xs, ys = [], []
+                    for t in range(tiles + 1):
+                        x = load(k - 1, part, t, r)
+                        above, below = load(k - 1, part, t, r, -1), load(k - 1, part, t, r, 1)
+                        twice = x + x
+                        xs.append(x if k == 1 else twice)
+                        ys.append(above + below + twice)
+                    left = [pltpu.roll(y, LANES - 1, 1) for y in ys]
+                    right = [pltpu.roll(y, 1, 1) for y in ys]
+                    out = []
+                    for t in range(tiles + 1 if k < KCHEB else tiles):
+                        y = (
+                            (ys[t] + ys[t])
+                            + jnp.where(last_lane, left[(t + 1) % (tiles + 1)], left[t])
+                            + jnp.where(first_lane, right[t - 1], right[t])
+                        )
+                        if k == 1:
+                            z = 0.125 * y - xs[t]
+                        else:
+                            z = 0.25 * y - (xs[t] + load(k - 2, part, t, r))
+                        if k < KCHEB:
+                            z = kept(z, r, t)
+                            store(k, part, t, r, z)
+                        out.append(z)
+                    new.append(out)
+                if r in centre:
+                    for t in range(tiles):
+                        add(k, t, r, (new[0][t], new[1][t]))
         for part in range(2):
             for t in range(tiles):
-                fields[d + 1, 2 * pair + part, t, pl.ds(HALO, rows)] = total[part][t]
+                for r in centre:
+                    fields[d + 1, 2 * pair + part, t, r:r + 8] = total[part][t, r]
 
     def image_copy(d, source, owner):
         return pltpu.make_async_remote_copy(
@@ -295,9 +328,8 @@
     bins = filter_table.shape[0]
     per = depths // freqs
     table = lax.dynamic_index_in_dim(filter_table, freq_pick[0], 1, keepdims=False)
-    table = jnp.transpose(table, (1, 2, 0)).reshape(1, ORDERS * 2 * bins)
-    wide = -(-table.shape[1] // LANES) * LANES
-    table = jnp.pad(table, ((0, 0), (0, wide - table.shape[1])))
+    table = jnp.transpose(table, (1, 2, 0)).reshape(ORDERS * 2, bins)
+    table = jnp.pad(table, ((0, 0), (0, LANES - bins)))
     vmem = pl.BlockSpec(memory_space=pltpu.VMEM)
     return pl.pallas_call(
         functools.partial(kernel, (lats, freqs, bins)),
@@ -313,13 +345,15 @@
             pltpu.VMEM((ORDERS * 2, tiles, rows, LANES), jnp.float32),
             pltpu.VMEM((depths, rows, cols), jnp.float32),
             pltpu.VMEM((depths, freqs, rows, cols), jnp.float32),
+            pltpu.VMEM((ORDERS * 4, 8, LANES), jnp.float32),
             pltpu.SemaphoreType.DMA((depths, 2, 5)),
             pltpu.SemaphoreType.DMA((depths, 2, 5)),
             pltpu.SemaphoreType.DMA((depths, freqs)),
             pltpu.SemaphoreType.DMA((depths, freqs)),
             pltpu.SemaphoreType.DMA((depths,)),
             pltpu.SemaphoreType.DMA((depths, freqs)),
-        ],
+        ]
+        + [pltpu.VMEM((rows + 2 * HALO + 24, LANES), jnp.float32)] * (6 * (tiles + 1)),
         compiler_params=pltpu.CompilerParams(
             collective_id=0, has_side_effects=True, vmem_limit_bytes=32 * 1024 * 1024
         ),

time: 32.2 us -> 30.3 us (0.941)
  Pallas kernels: 27.8 us -> 25.9 us
    pallas_call x1, Pallas kernels: 27.8 us -> 25.9 us  [body(): pl.pallas_call(functools.partial(kernel, (lats, freqs, bins)), out_shape=...]
where the time goes in v3:
time: 30.3 us; the launch traced here: 30.2 us
  Pallas kernels  25.9 us (85%)
  local copies, waits for them, and re-layouts  2.87 us (9%)
  between operations  1.38 us (5%)
    pallas_call x1, Pallas kernels, body(): pl.pallas_call(functools.partial(kernel, (lats, freqs, bins)), out_shape=...  25.9 us
    unnamed x10, local copies, waits for them, and re-layouts  2.3 us

profile of v3, /device:TPU:0, one launch (start us, length us, event | category | flops | bytes accessed | tf_op | source)
XLA Modules:
  0.0 30.2 jit_solution(9258085058545762865)
XLA Ops:
  0.6 0.0 copy-start
  1.3 0.3 copy-done
  1.6 0.4 %constant_dynamic-slice_fusion = f32[32,1,9,2]{1,3,2,0:T(2,128)S(1)} fusion(f32[32,32,9,2]{1,3,2,0:T(2,128)S(1)} %copy-done, s32[]{:T(128)S(6)} %select_n.4), kind=kLoop, calls=%fused_computation | loop fusion | bytes 4612 | tf_op jit(solution)/shard_map/jit(dynamic_index_in_dim)/dynamic_slice | solution.py:330
  2.0 0.0 copy-start.1
  2.0 0.0 copy-start.2
  2.0 0.2 copy.7
  2.2 0.0 copy-start.3
  2.2 0.7 %copy-done.1 = f32[1,4,16,512]{3,2,1,0:T(8,128)S(1)} copy-done((f32[1,4,16,512]{3,2,1,0:T(8,128)S(1)}, f32[1,4,16,512]{3,2,1,0:T(8,128)}, u32[]{:S(2)}) %copy-start.1) | copy-done | bytes 131096
  2.9 0.1 copy-done.2
  3.0 0.0 copy-done.3
  3.0 25.9 %shard_map.68 = (f32[1,4,16,512]{3,2,1,0:T(8,128)S(1)}, f32[2,16,512]{2,1,0:T(8,128)S(1)}) custom-call(f32[1,4,16,512]{3,2,1,0:T(8,128)S(1)} %copy-done.1, f32[4,16,512]{2,1,0:T(8,128)S(1)} %copy-done.2, f32[18,128]{1,0:T(8,128)S(1)} %pad.4.tab_ref, s32[4]{0:T(128)S(1)} %copy-done.3), custom_call_target="tpu_custom_call" | custom-call | tf_op jit(solution)/shard_map/pallas_call | solution.py:334
  28.9 0.7 %copy.11 = f32[1,4,16,512]{3,2,1,0:T(8,128)} copy(f32[1,4,16,512]{3,2,1,0:T(8,128)S(1)} %get-tuple-element.4) | data formatting | bytes 262144
  29.5 0.6 %copy.12 = f32[2,16,512]{2,1,0:T(8,128)} copy(f32[2,16,512]{2,1,0:T(8,128)S(1)} %get-tuple-element.5) | data formatting | bytes 131072
  (2 shorter events, 0.0 us)
Async XLA Ops:
  0.6 1.0 %copy-start = (f32[32,32,9,2]{1,3,2,0:T(2,128)S(1)}, f32[32,32,9,2]{1,3,2,0:T(2,128)}, u32[]{:S(2)}) copy-start(f32[32,32,9,2]{1,3,2,0:T(2,128)} %param.7) | copy-start | bytes 221188
  2.0 0.9 %copy-start.1 = (f32[1,4,16,512]{3,2,1,0:T(8,128)S(1)}, f32[1,4,16,512]{3,2,1,0:T(8,128)}, u32[]{:S(2)}) copy-start(f32[1,4,16,512]{3,2,1,0:T(8,128)} %wave_ref.1) | copy-start | bytes 393220
  2.0 1.0 %copy-start.2 = (f32[4,16,512]{2,1,0:T(8,128)S(1)}, f32[4,16,512]{2,1,0:T(8,128)}, u32[]{:S(2)}) copy-start(f32[4,16,512]{2,1,0:T(8,128)} %vel_ref.1) | copy-start | bytes 393220
  2.2 0.7 %copy-start.3 = (s32[4]{0:T(128)S(1)}, s32[4]{0:T(128)}, u32[]{:S(2)}) copy-start(s32[4]{0:T(128)} %slab_ref.1) | copy-start | bytes 52

commit v4 on v3

--- a/solution.py
+++ b/solution.py
@@ -15,7 +15,7 @@
 
 
 def kernel(sizes, wave_ref, vel_ref, tab_ref, slab_ref, out_ref, image_ref,
-           fields, slots, coef, partial, arrived, tables,
+           fields, slots, coef, partial, arrived, spread, stored, load_sem,
            halo_send, halo_recv, vel_send, vel_recv, img_send, img_recv, *work):
     lats, freqs, bins = sizes
     depths = slab_ref.shape[0]
@@ -23,6 +23,8 @@
     tiles = cols // LANES
     per = image_ref.shape[0]
     tall = rows + 2 * HALO
+    wide = ORDERS * 2 * 8
+    chunk = min(256, cols)
     lat = lax.axis_index("lat")
     sub = lax.axis_index("sub")
     freq = lax.axis_index("freq")
@@ -125,11 +127,21 @@
 
         halo_copy(d, pair, 2).wait_send()
 
+    loads = [
+        pltpu.make_async_copy(
+            wave_ref.at[0, :, :, pl.ds(t * LANES, LANES)],
+            fields.at[0, :, t, pl.ds(HALO, rows)],
+            load_sem.at[t],
+        )
+        for t in range(tiles)
+    ]
+    loads.append(pltpu.make_async_copy(vel_ref, stored, load_sem.at[tiles]))
+    for copy in loads:
+        copy.start()
+    for copy in loads:
+        copy.wait()
     for d in range(depths):
-        slots[d, freq] = vel_ref[slab_ref[d] % slab_size]
-    for part in range(4):
-        for t in range(tiles):
-            fields[0, part, t, pl.ds(HALO, rows)] = wave_ref[0, part, :, t * LANES:(t + 1) * LANES]
+        slots[d, freq] = stored[slab_ref[d] % slab_size]
     pl.semaphore_wait(
         barrier, freqs + jnp.where(has_up, 2, 0) + jnp.where(has_down, 2, 0)
     )
@@ -141,11 +153,27 @@
     for d in range(1, depths):
         for step in range(1, freqs):
             vel_copy(d, freq, lax.rem(freq + step, freqs)).start()
-    bin_id = lax.broadcasted_iota(jnp.int32, (8, LANES), 1)
-    for j in range(ORDERS * 2):
-        low = jnp.broadcast_to(tab_ref[j:j + 1], (8, LANES))
-        tables[2 * j] = low
-        tables[2 * j + 1] = jnp.where(bin_id < bins - 1, pltpu.roll(low, LANES - 1, 1) - low, 0.0)
+    def one_hot(shape, row_step, col_step):
+        i = lax.broadcasted_iota(jnp.int32, shape, 0) // row_step
+        j = lax.broadcasted_iota(jnp.int32, shape, 1) // col_step
+        return (i == j).astype(jnp.float32)
+
+    tall_table = jnp.dot(
+        one_hot((wide, ORDERS * 2), 8, 1), tab_ref[...],
+        precision=lax.Precision.HIGHEST, preferred_element_type=jnp.float32,
+    )
+    full = jnp.dot(
+        tall_table, one_hot((bins, bins * 8), 1, 8),
+        precision=lax.Precision.HIGHEST, preferred_element_type=jnp.float32,
+    )
+    same_row = (
+        lax.broadcasted_iota(jnp.int32, full.shape, 0) % 8
+        == lax.broadcasted_iota(jnp.int32, full.shape, 1) % 8
+    )
+    full = jnp.where(same_row, full, 0.0)
+    high_part = full.astype(jnp.bfloat16)
+    spread[:wide] = high_part
+    spread[wide:] = (full - high_part.astype(jnp.float32)).astype(jnp.bfloat16)
 
     lane = lax.broadcasted_iota(jnp.int32, (tall, LANES), 1)
     row = lax.broadcasted_iota(jnp.int32, (tall, LANES), 0)
@@ -162,19 +190,24 @@
             source = lax.rem(freq + step, freqs)
             vel_copy(d, source, source).wait_recv()
         owner = slab_ref[d] // slab_size
-        for t in range(tiles):
-            for r in range(0, rows, 8):
-                v = jnp.zeros((8, LANES), jnp.float32)
+        for r in range(0, rows, 8):
+            for c in range(0, cols, chunk):
+                v = jnp.zeros((8, chunk), jnp.float32)
                 for source in range(freqs):
-                    block = slots[d, source, r:r + 8, t * LANES:(t + 1) * LANES]
-                    v = jnp.where(owner == source, block, v)
-                base = jnp.floor(v)
-                upper = v - base
-                index = jnp.clip(base.astype(jnp.int32), 0, bins - 1)
+                    v = jnp.where(owner == source, slots[d, source, r:r + 8, c:c + chunk], v)
+                hats = jnp.concatenate(
+                    [jnp.maximum(0.0, 1.0 - jnp.abs(v - float(i))) for i in range(bins)], axis=0
+                )
+                high = hats.astype(jnp.bfloat16)
+                low = (hats - high.astype(jnp.float32)).astype(jnp.bfloat16)
+                both = jnp.dot(spread[...], high, preferred_element_type=jnp.float32)
+                rest = jnp.dot(spread[:wide], low, preferred_element_type=jnp.float32)
+                out = both[:wide] + (both[wide:] + rest)
                 for j in range(ORDERS * 2):
-                    low = jnp.take_along_axis(tables[2 * j], index, axis=1, mode="promise_in_bounds")
-                    rise = jnp.take_along_axis(tables[2 * j + 1], index, axis=1, mode="promise_in_bounds")
-                    coef[j, t, pl.ds(r, 8)] = low + upper * rise
+                    for t in range(chunk // LANES):
+                        coef[j, c // LANES + t, pl.ds(r, 8)] = out[
+                            8 * j:8 * j + 8, t * LANES:(t + 1) * LANES
+                        ]
 
     def kept(x, r, t):
         rows_here = slice(r, r + 8)
@@ -329,15 +362,15 @@
     per = depths // freqs
     table = lax.dynamic_index_in_dim(filter_table, freq_pick[0], 1, keepdims=False)
     table = jnp.transpose(table, (1, 2, 0)).reshape(ORDERS * 2, bins)
-    table = jnp.pad(table, ((0, 0), (0, LANES - bins)))
     vmem = pl.BlockSpec(memory_space=pltpu.VMEM)
+    hbm = pl.BlockSpec(memory_space=pltpu.HBM)
     return pl.pallas_call(
         functools.partial(kernel, (lats, freqs, bins)),
         out_shape=(
             jax.ShapeDtypeStruct(wavefields.shape, jnp.float32),
             jax.ShapeDtypeStruct((per, rows, cols), jnp.float32),
         ),
-        in_specs=[vmem, vmem, vmem, pl.BlockSpec(memory_space=pltpu.SMEM)],
+        in_specs=[hbm, hbm, vmem, pl.BlockSpec(memory_space=pltpu.SMEM)],
         out_specs=(vmem, vmem),
         scratch_shapes=[
             pltpu.VMEM((depths + 1, parts, tiles + 1, rows + 2 * HALO, LANES), jnp.float32),
@@ -345,7 +378,9 @@
             pltpu.VMEM((ORDERS * 2, tiles, rows, LANES), jnp.float32),
             pltpu.VMEM((depths, rows, cols), jnp.float32),
             pltpu.VMEM((depths, freqs, rows, cols), jnp.float32),
-            pltpu.VMEM((ORDERS * 4, 8, LANES), jnp.float32),
+            pltpu.VMEM((ORDERS * 2 * 8 * 2, bins * 8), jnp.bfloat16),
+            pltpu.VMEM(velocity.shape, jnp.float32),
+            pltpu.SemaphoreType.DMA((tiles + 1,)),
             pltpu.SemaphoreType.DMA((depths, 2, 5)),
             pltpu.SemaphoreType.DMA((depths, 2, 5)),
             pltpu.SemaphoreType.DMA((depths, freqs)),

time: 30.3 us -> 30.4 us (level)
  no operation moved by 1% of the time
where the time goes in v4:
time: 30.4 us; the launch traced here: 30.3 us
  Pallas kernels  26 us (86%)
  local copies, waits for them, and re-layouts  2.88 us (9%)
  between operations  1.38 us (5%)
    pallas_call x1, Pallas kernels, body(): pl.pallas_call(functools.partial(kernel, (lats, freqs, bins)), out_shape=...  26 us
    unnamed x10, local copies, waits for them, and re-layouts  2.32 us

profile of v4, /device:TPU:0, one launch (start us, length us, event | category | flops | bytes accessed | tf_op | source)
XLA Modules:
  0.0 30.3 jit_solution(14900923550021639997)
XLA Ops:
  0.6 0.0 copy-start
  1.3 0.3 copy-done
  1.6 0.4 %constant_dynamic-slice_fusion = f32[32,1,9,2]{1,3,2,0:T(2,128)S(1)} fusion(f32[32,32,9,2]{1,3,2,0:T(2,128)S(1)} %copy-done, s32[]{:T(128)S(6)} %select_n.4), kind=kLoop, calls=%fused_computation | loop fusion | bytes 4612 | tf_op jit(solution)/shard_map/jit(dynamic_index_in_dim)/dynamic_slice | solution.py:363
  2.0 0.0 copy-start.1
  2.0 0.0 copy-start.2
  2.0 0.2 copy.7
  2.2 0.0 copy-start.3
  2.2 0.7 %copy-done.1 = f32[1,4,16,512]{3,2,1,0:T(8,128)S(1)} copy-done((f32[1,4,16,512]{3,2,1,0:T(8,128)S(1)}, f32[1,4,16,512]{3,2,1,0:T(8,128)}, u32[]{:S(2)}) %copy-start.1) | copy-done | bytes 131096
  2.9 0.1 copy-done.2
  3.0 0.0 copy-done.3
  3.0 26.0 %shard_map.68 = (f32[1,4,16,512]{3,2,1,0:T(8,128)S(1)}, f32[2,16,512]{2,1,0:T(8,128)S(1)}) custom-call(f32[1,4,16,512]{3,2,1,0:T(8,128)S(1)} %copy-done.1, f32[4,16,512]{2,1,0:T(8,128)S(1)} %copy-done.2, f32[18,32]{1,0:T(8,128)S(1)} %reshape.7.tab_ref, s32[4]{0:T(128)S(1)} %copy-done.3), custom_call_target="tpu_custom_call" | custom-call | tf_op jit(solution)/shard_map/pallas_call | solution.py:367
  29.0 0.7 %copy.11 = f32[1,4,16,512]{3,2,1,0:T(8,128)} copy(f32[1,4,16,512]{3,2,1,0:T(8,128)S(1)} %get-tuple-element.4) | data formatting | bytes 262144
  29.7 0.6 %copy.12 = f32[2,16,512]{2,1,0:T(8,128)} copy(f32[2,16,512]{2,1,0:T(8,128)S(1)} %get-tuple-element.5) | data formatting | bytes 131072
  (1 shorter events, 0.0 us)
Async XLA Ops:
  0.6 1.0 %copy-start = (f32[32,32,9,2]{1,3,2,0:T(2,128)S(1)}, f32[32,32,9,2]{1,3,2,0:T(2,128)}, u32[]{:S(2)}) copy-start(f32[32,32,9,2]{1,3,2,0:T(2,128)} %param.7) | copy-start | bytes 221188
  2.0 0.9 %copy-start.1 = (f32[1,4,16,512]{3,2,1,0:T(8,128)S(1)}, f32[1,4,16,512]{3,2,1,0:T(8,128)}, u32[]{:S(2)}) copy-start(f32[1,4,16,512]{3,2,1,0:T(8,128)} %wave_ref.1) | copy-start | bytes 393220
  2.0 1.0 %copy-start.2 = (f32[4,16,512]{2,1,0:T(8,128)S(1)}, f32[4,16,512]{2,1,0:T(8,128)}, u32[]{:S(2)}) copy-start(f32[4,16,512]{2,1,0:T(8,128)} %vel_ref.1) | copy-start | bytes 393220
  2.2 0.8 %copy-start.3 = (s32[4]{0:T(128)S(1)}, s32[4]{0:T(128)}, u32[]{:S(2)}) copy-start(s32[4]{0:T(128)} %slab_ref.1) | copy-start | bytes 52

commit v5 on v4

v5 whole, which is shorter than its diff:
```python
import functools

import jax
import jax.numpy as jnp
from jax import lax
from jax.experimental import pallas as pl
from jax.experimental.pallas import tpu as pltpu
from jax.sharding import PartitionSpec as P

KCHEB = 8
ORDERS = KCHEB + 1
HALO = 8
WIDE_HALO = 16
LANES = 128
MESH = pl.DeviceIdType.MESH


def kernel(sizes, wave_ref, vel_ref, tab_ref, slab_ref, out_ref, image_ref,
           fields, middle, slots, coef_first, coef_second, partial, arrived, spread, stored, load_sem,
           halo_send, halo_recv, vel_send, vel_recv, img_send, img_recv, *work):
    lats, freqs, bins = sizes
    depths = slab_ref.shape[0]
    slab_size, rows, cols = vel_ref.shape
    tiles = cols // LANES
    per = image_ref.shape[0]
    rounds = depths // 2
    wide = ORDERS * 2 * 8
    lat = lax.axis_index("lat")
    sub = lax.axis_index("sub")
    freq = lax.axis_index("freq")
    has_up = lat > 0
    has_down = lat < lats - 1
    other = 1 - sub
    edge_tile = (tiles - 1) * (1 - sub)

    barrier = pltpu.get_barrier_semaphore()

    def greet_row(target):
        for step in range(freqs):
            place = dict(target, freq=lax.rem(freq + step, freqs))
            if step > 0 or target:
                pl.semaphore_signal(barrier, inc=1, device_id=place, device_id_type=MESH)
            pl.semaphore_signal(
                barrier, inc=1, device_id=dict(place, sub=other), device_id_type=MESH
            )

    greet_row({})

    @pl.when(has_up)
    def _():
        greet_row({"lat": lat - 1})

    @pl.when(has_down)
    def _():
        greet_row({"lat": lat + 1})

    loads = [
        pltpu.make_async_copy(
            wave_ref.at[0, :, :, pl.ds(t * LANES, LANES)],
            fields.at[0, :, t, pl.ds(WIDE_HALO, rows)],
            load_sem.at[t],
        )
        for t in range(tiles)
    ]
    loads.append(pltpu.make_async_copy(vel_ref, stored, load_sem.at[tiles]))
    for copy in loads:
        copy.start()
    for copy in loads:
        copy.wait()
    for d in range(depths):
        row_here = stored[slab_ref[d] % slab_size]
        for t in range(tiles):
            slots[d, freq, t, pl.ds(HALO, rows)] = row_here[:, t * LANES:(t + 1) * LANES]
    pl.semaphore_wait(
        barrier, 2 * freqs * (1 + jnp.where(has_up, 1, 0) + jnp.where(has_down, 1, 0)) - 1
    )

    def place_of(way, halo):
        src_rows = (halo, rows, halo, halo, rows, halo)[way]
        dst_rows = (halo + rows, 0, halo, halo + rows, 0, halo)[way]
        count = rows if way in (2, 5) else halo
        if way in (0, 1, 5):
            src_tiles, dst_tiles = pl.ds(0, tiles), pl.ds(0, tiles)
        else:
            src_tiles, dst_tiles = pl.ds(edge_tile, 1), pl.ds(tiles, 1)
        target = {}
        if way in (0, 3):
            target["lat"] = lat - 1
        if way in (1, 4):
            target["lat"] = lat + 1
        if way in (2, 3, 4):
            target["sub"] = other
        return (src_tiles, pl.ds(src_rows, count)), (dst_tiles, pl.ds(dst_rows, count)), target

    def vel_copy(d, source, target, way):
        src, dst, place = place_of(way, HALO)
        return pltpu.make_async_remote_copy(
            src_ref=slots.at[d, source, *src],
            dst_ref=slots.at[d, source, *dst],
            send_sem=vel_send.at[d, target, way],
            recv_sem=vel_recv.at[d, source, way],
            device_id=dict(place, freq=target),
            device_id_type=MESH,
        )

    def halo_copy(e, pair, way):
        src, dst, place = place_of(way, WIDE_HALO)
        parts = pl.ds(2 * pair, 2)
        return pltpu.make_async_remote_copy(
            src_ref=fields.at[e, parts, *src],
            dst_ref=fields.at[e, parts, *dst],
            send_sem=halo_send.at[e, pair, way],
            recv_sem=halo_recv.at[e, pair, way],
            device_id=place,
            device_id_type=MESH,
        )

    def all_ways(do):
        @pl.when(has_up)
        def _():
            do(0)
            do(3)

        @pl.when(has_down)
        def _():
            do(1)
            do(4)

        do(2)

    def all_ways_in(do):
        @pl.when(has_down)
        def _():
            do(0)
            do(3)

        @pl.when(has_up)
        def _():
            do(1)
            do(4)

        do(2)

    def each_velocity(d, do):
        for step in range(freqs):
            target = lax.rem(freq + step, freqs)
            if step > 0:
                do(vel_copy(d, freq, target, 5))
            if d % 2 == 0:
                all_ways(lambda way: do(vel_copy(d, freq, target, way)))

    def send_halo(e, pair):
        all_ways(lambda way: halo_copy(e, pair, way).start())

    def wait_halo(e, pair):
        all_ways_in(lambda way: halo_copy(e, pair, way).wait_recv())

    each_velocity(0, lambda copy: copy.start())
    for pair in range(2):
        send_halo(0, pair)
    for d in range(1, depths):
        each_velocity(d, lambda copy: copy.start())
    def one_hot(shape, row_step, col_step):
        i = lax.broadcasted_iota(jnp.int32, shape, 0) // row_step
        j = lax.broadcasted_iota(jnp.int32, shape, 1) // col_step
        return (i == j).astype(jnp.float32)

    tall_table = jnp.dot(
        one_hot((wide, ORDERS * 2), 8, 1), tab_ref[...],
        precision=lax.Precision.HIGHEST, preferred_element_type=jnp.float32,
    )
    full = jnp.dot(
        tall_table, one_hot((bins, bins * 8), 1, 8),
        precision=lax.Precision.HIGHEST, preferred_element_type=jnp.float32,
    )
    same_row = (
        lax.broadcasted_iota(jnp.int32, full.shape, 0) % 8
        == lax.broadcasted_iota(jnp.int32, full.shape, 1) % 8
    )
    full = jnp.where(same_row, full, 0.0)
    high_part = full.astype(jnp.bfloat16)
    spread[:wide] = high_part
    spread[wide:] = (full - high_part.astype(jnp.float32)).astype(jnp.bfloat16)

    lane = lax.broadcasted_iota(jnp.int32, (8, LANES), 1)
    lane_low = jnp.where(sub == 0, 0, LANES // 2)
    side = (lane >= lane_low) & (lane < lane_low + LANES // 2)
    everywhere = lane >= 0
    above = everywhere & (jnp.where(has_up, 1, 0) > 0)
    below = everywhere & (jnp.where(has_down, 1, 0) > 0)
    first_lane = lane == 0
    last_lane = lane == LANES - 1

    def make_coefficients(d, first):
        coef = coef_first if first else coef_second
        owner = slab_ref[d] // slab_size
        blocks = range(0, rows + 2 * HALO, 8) if first else range(HALO, HALO + rows, 8)
        for r in blocks:
            for t0 in range(0, tiles + 1 if first else tiles, 2):
                pieces = range(t0, min(t0 + 2, tiles + 1 if first else tiles))
                views = []
                for t in pieces:
                    v = jnp.zeros((8, LANES), jnp.float32)
                    for source in range(freqs):
                        v = jnp.where(owner == source, slots[d, source, t, r:r + 8], v)
                    views.append(v)
                v = jnp.concatenate(views, axis=1)
                hats = jnp.concatenate(
                    [jnp.maximum(0.0, 1.0 - jnp.abs(v - float(i))) for i in range(bins)], axis=0
                )
                high = hats.astype(jnp.bfloat16)
                low = (hats - high.astype(jnp.float32)).astype(jnp.bfloat16)
                both = jnp.dot(spread[...], high, preferred_element_type=jnp.float32)
                rest = jnp.dot(spread[:wide], low, preferred_element_type=jnp.float32)
                out = both[:wide] + (both[wide:] + rest)
                for j in range(ORDERS * 2):
                    for t in pieces:
                        coef[j, t, pl.ds(r, 8)] = out[
                            8 * j:8 * j + 8, (t - t0) * LANES:(t - t0 + 1) * LANES
                        ]

    def wait_velocity(d, first):
        for step in range(freqs):
            source = lax.rem(freq + step, freqs)
            if step > 0:
                vel_copy(d, source, source, 5).wait_recv()
            if first:
                all_ways_in(lambda way: vel_copy(d, source, source, way).wait_recv())

    def propagate(e, pair, first):
        shift = lax.rem(e, 2) * 8
        halo = WIDE_HALO if first else HALO
        tall = rows + 2 * halo
        out_tiles = tiles + 1 if first else tiles
        coef = coef_first if first else coef_second
        coef_row = 0 if first else HALO

        def kept(x, r, t):
            inside = side if t == tiles else None
            if r < halo:
                inside = above if inside is None else inside & above
            if r >= halo + rows:
                inside = below if inside is None else inside & below
            return x if inside is None else jnp.where(inside, x, 0.0)

        def load(k, part, t, r, off=0):
            start = shift + (8 + r + off)
            if off == 0:
                start = pl.multiple_of(start, 8)
            return work[((k % 3) * 2 + part) * (tiles + 1) + t][pl.ds(start, 8)]

        def store(k, part, t, r, x):
            start = pl.multiple_of(shift + (8 + r), 8)
            work[((k % 3) * 2 + part) * (tiles + 1) + t][pl.ds(start, 8)] = x

        blocks = range(0, tall, 8)
        centre = range(HALO, tall - HALO, 8)
        total = [{} for _ in range(2)]

        def add(k, t, r, now):
            a = coef[2 * k, t, pl.ds(r - HALO + coef_row, 8)]
            b = coef[2 * k + 1, t, pl.ds(r - HALO + coef_row, 8)]
            p, q = now
            if pair == 0:
                add0, add1 = a * p + b * q, a * q - b * p
            else:
                add0, add1 = a * p - b * q, a * q + b * p
            total[0][t, r] = add0 if k == 0 else total[0][t, r] + add0
            total[1][t, r] = add1 if k == 0 else total[1][t, r] + add1

        for r in blocks:
            for t in range(tiles + 1):
                now = []
                for part in range(2):
                    if first:
                        x = fields[e, 2 * pair + part, t, r:r + 8]
                    else:
                        x = middle[2 * pair + part, t, r:r + 8]
                    x = kept(x, r, t)
                    store(0, part, t, r, x)
                    now.append(x)
                if t < out_tiles and r in centre:
                    add(0, t, r, now)
        for k in range(1, ORDERS):
            for r in blocks if k < KCHEB else centre:
                new = []
                for part in range(2):
                    xs, ys = [], []
                    for t in range(tiles + 1):
                        x = load(k - 1, part, t, r)
                        upper, lower = load(k - 1, part, t, r, -1), load(k - 1, part, t, r, 1)
                        twice = x + x
                        xs.append(x if k == 1 else twice)
                        ys.append(upper + lower + twice)
                    left = [pltpu.roll(y, LANES - 1, 1) for y in ys]
                    right = [pltpu.roll(y, 1, 1) for y in ys]
                    out = []
                    for t in range(tiles + 1 if k < KCHEB else out_tiles):
                        y = (
                            (ys[t] + ys[t])
                            + jnp.where(last_lane, left[(t + 1) % (tiles + 1)], left[t])
                            + jnp.where(first_lane, right[t - 1], right[t])
                        )
                        if k == 1:
                            z = 0.125 * y - xs[t]
                        else:
                            z = 0.25 * y - (xs[t] + load(k - 2, part, t, r))
                        if k < KCHEB:
                            z = kept(z, r, t)
                            store(k, part, t, r, z)
                        out.append(z)
                    new.append(out)
                if r in centre:
                    for t in range(out_tiles):
                        add(k, t, r, (new[0][t], new[1][t]))
        for part in range(2):
            for t in range(out_tiles):
                for r in centre:
                    if first:
                        middle[2 * pair + part, t, pl.ds(r - HALO, 8)] = total[part][t, r]
                    else:
                        fields[e + 1, 2 * pair + part, t, pl.ds(r + HALO, 8)] = total[part][t, r]

    def image_copy(d, source, owner):
        return pltpu.make_async_remote_copy(
            src_ref=partial.at[d],
            dst_ref=arrived.at[d, source],
            send_sem=img_send.at[d],
            recv_sem=img_recv.at[d, source],
            device_id={"freq": owner},
            device_id_type=MESH,
        )

    def coefficients_of(e):
        for first in (True, False):
            wait_velocity(2 * e + (0 if first else 1), first)
            make_coefficients(2 * e + (0 if first else 1), first)

    def make_image(d, cells):
        for t in range(tiles):
            u = [cells(part, t) for part in range(4)]
            partial[d, :, t * LANES:(t + 1) * LANES] = u[0] * u[2] + u[1] * u[3]
        owner = d // per

        @pl.when(owner != freq)
        def _():
            image_copy(d, freq, owner).start()

    coefficients_of(0)

    def round_step(e, carry):
        for pair in range(2):
            wait_halo(e, pair)
            propagate(e, pair, True)
            propagate(e, pair, False)

            @pl.when(e < rounds - 1)
            def _():
                send_halo(e + 1, pair)

        make_image(2 * e, lambda part, t: middle[part, t, pl.ds(HALO, rows)])
        make_image(2 * e + 1, lambda part, t: fields[e + 1, part, t, pl.ds(WIDE_HALO, rows)])

        @pl.when(e < rounds - 1)
        def _():
            coefficients_of(e + 1)

        return carry

    lax.fori_loop(0, rounds, round_step, 0)

    for part in range(4):
        for t in range(tiles):
            out_ref[0, part, :, t * LANES:(t + 1) * LANES] = fields[rounds, part, t, pl.ds(WIDE_HALO, rows)]

    for i in range(per):
        d = freq * per + i
        total = partial[d]
        for step in range(1, freqs):
            source = lax.rem(freq + step, freqs)
            image_copy(d, source, source).wait_recv()
            total = total + arrived[d, source]
        image_ref[i] = total

    for e in range(rounds):
        for pair in range(2):
            all_ways(lambda way: halo_copy(e, pair, way).wait_send())
    for d in range(depths):
        each_velocity(d, lambda copy: copy.wait_send())

        @pl.when(d // per != freq)
        def _():
            image_copy(d, freq, d // per).wait_send()


def body(sizes, wavefields, velocity, filter_table, freq_pick, slab_order):
    lats, freqs = sizes
    depths = slab_order.shape[0]
    _, parts, rows, cols = wavefields.shape
    tiles = cols // LANES
    bins = filter_table.shape[0]
    per = depths // freqs
    rounds = depths // 2
    table = lax.dynamic_index_in_dim(filter_table, freq_pick[0], 1, keepdims=False)
    table = jnp.transpose(table, (1, 2, 0)).reshape(ORDERS * 2, bins)
    vmem = pl.BlockSpec(memory_space=pltpu.VMEM)
    hbm = pl.BlockSpec(memory_space=pltpu.HBM)
    return pl.pallas_call(
        functools.partial(kernel, (lats, freqs, bins)),
        out_shape=(
            jax.ShapeDtypeStruct(wavefields.shape, jnp.float32),
            jax.ShapeDtypeStruct((per, rows, cols), jnp.float32),
        ),
        in_specs=[hbm, hbm, vmem, pl.BlockSpec(memory_space=pltpu.SMEM)],
        out_specs=(vmem, vmem),
        scratch_shapes=[
            pltpu.VMEM((rounds + 1, parts, tiles + 1, rows + 2 * WIDE_HALO, LANES), jnp.float32),
            pltpu.VMEM((parts, tiles + 1, rows + 2 * HALO, LANES), jnp.float32),
            pltpu.VMEM((depths, freqs, tiles + 1, rows + 2 * HALO, LANES), jnp.float32),
            pltpu.VMEM((ORDERS * 2, tiles + 1, rows + 2 * HALO, LANES), jnp.float32),
            pltpu.VMEM((ORDERS * 2, tiles + 1, rows + 2 * HALO, LANES), jnp.float32),
            pltpu.VMEM((depths, rows, cols), jnp.float32),
            pltpu.VMEM((depths, freqs, rows, cols), jnp.float32),
            pltpu.VMEM((ORDERS * 2 * 8 * 2, bins * 8), jnp.bfloat16),
            pltpu.VMEM(velocity.shape, jnp.float32),
            pltpu.SemaphoreType.DMA((tiles + 1,)),
            pltpu.SemaphoreType.DMA((rounds, 2, 5)),
            pltpu.SemaphoreType.DMA((rounds, 2, 5)),
            pltpu.SemaphoreType.DMA((depths, freqs, 6)),
            pltpu.SemaphoreType.DMA((depths, freqs, 6)),
            pltpu.SemaphoreType.DMA((depths,)),
            pltpu.SemaphoreType.DMA((depths, freqs)),
        ]
        + [pltpu.VMEM((rows + 2 * WIDE_HALO + 24, LANES), jnp.float32)] * (6 * (tiles + 1)),
        compiler_params=pltpu.CompilerParams(
            collective_id=0, has_side_effects=True, vmem_limit_bytes=56 * 1024 * 1024
        ),
    )(wavefields, velocity, table, slab_order)


def solution(mesh):
    sizes = (mesh.shape["lat"], mesh.shape["freq"])
    return jax.shard_map(
        functools.partial(body, sizes),
        mesh=mesh,
        in_specs=(
            P(("shots", "freq"), None, "lat", "sub"),
            P("freq", "lat", "sub"),
            P(),
            P("freq"),
            P(),
        ),
        out_specs=(P(("shots", "freq"), None, "lat", "sub"), P(("shots", "freq"), "lat", "sub")),
        check_vma=False,
    )
```

time: 30.4 us -> 32 us (1.053)
  local copies, waits for them, and re-layouts: 2.88 us -> 3.69 us
  Pallas kernels: 26 us -> 26.7 us
    pallas_call x1, Pallas kernels: 26 us -> 26.7 us  [body(): pl.pallas_call(functools.partial(kernel, (lats, freqs, bins)), out_shape=...]
    reshape x1, local copies, waits for them, and re-layouts: 0.02 us -> 0.64 us  [body(): table = jnp.transpose(table, (1, 2, 0)).reshape(ORDERS * 2, bins)]
    unnamed x10 -> x6, local copies, waits for them, and re-layouts: 2.32 us -> 2.51 us
where the time goes in v5:
time: 32 us; the launch traced here: 31.8 us
  Pallas kernels  26.7 us (83%)
  local copies, waits for them, and re-layouts  3.69 us (12%)
  between operations  1.36 us (4%)
    pallas_call x1, Pallas kernels, body(): pl.pallas_call(functools.partial(kernel, (lats, freqs, bins)), out_shape=...  26.7 us
    unnamed x6, local copies, waits for them, and re-layouts  2.51 us

profile of v5, /device:TPU:0, one launch (start us, length us, event | category | flops | bytes accessed | tf_op | source)
XLA Modules:
  0.0 31.8 jit_solution(16107650181630442200)
XLA Ops:
  0.6 0.0 copy-start
  1.3 0.3 copy-done
  1.6 0.4 %constant_dynamic-slice_fusion = f32[32,1,9,2]{1,3,2,0:T(2,128)S(1)} fusion(f32[32,32,9,2]{1,3,2,0:T(2,128)S(1)} %copy-done, s32[]{:T(128)S(6)} %select_n.4), kind=kLoop, calls=%fused_computation | loop fusion | bytes 4612 | tf_op jit(solution)/shard_map/jit(dynamic_index_in_dim)/dynamic_slice | solution.py:404
  2.0 0.2 copy.7
  2.2 0.6 %reshape.7.tab_ref = f32[18,32]{1,0:T(8,128)} reshape(f32[9,2,32]{2,1,0:T(2,128)S(1)} %bitcast.7) | data formatting | bytes 4608 | tf_op jit(solution)/shard_map/reshape | solution.py:405
  2.8 26.7 %shard_map.68 = (f32[1,4,16,512]{3,2,1,0:T(8,128)}, f32[2,16,512]{2,1,0:T(8,128)}) custom-call(f32[1,4,16,512]{3,2,1,0:T(8,128)} %wave_ref.1, f32[4,16,512]{2,1,0:T(8,128)} %vel_ref.1, f32[18,32]{1,0:T(8,128)} %reshape.7.tab_ref, s32[4]{0:T(128)} %slab_ref.1), custom_call_target="tpu_custom_call" | custom-call | tf_op jit(solution)/shard_map/pallas_call | solution.py:408
  29.5 0.0 copy-start.1
  29.5 1.6 %copy.11 = f32[1,4,16,512]{3,2,1,0:T(8,128)} copy(f32[1,4,16,512]{3,2,1,0:T(8,128)} %get-tuple-element.4) | data formatting | bytes 262144
  31.1 0.0 copy-done.1
  31.1 0.6 %copy.12 = f32[2,16,512]{2,1,0:T(8,128)} copy(f32[2,16,512]{2,1,0:T(8,128)S(1)} %copy-done.1) | data formatting | bytes 131072
Async XLA Ops:
  0.6 1.0 %copy-start = (f32[32,32,9,2]{1,3,2,0:T(2,128)S(1)}, f32[32,32,9,2]{1,3,2,0:T(2,128)}, u32[]{:S(2)}) copy-start(f32[32,32,9,2]{1,3,2,0:T(2,128)} %param.7) | copy-start | bytes 221188
  29.5 1.6 %copy-start.1 = (f32[2,16,512]{2,1,0:T(8,128)S(1)}, f32[2,16,512]{2,1,0:T(8,128)}, u32[]{:S(2)}) copy-start(f32[2,16,512]{2,1,0:T(8,128)} %get-tuple-element.5) | copy-start | bytes 196612
